TPU v7x, 128 devices: a whole 4x4x4 slice. The times are simulated.
128 devices in a mesh: fsdp: 4 (over x_lo, core), ctx: 32 (over z, y, x_hi).
Axes of the slice: x: 4 (x_hi: 2, x_lo: 2; x = x_hi * 2 + x_lo), y: 4, z: 4, core: 2. Of those that a mesh axis runs over, the one named last changes fastest.
Arguments:
- tokens: bfloat16 [16384, 1024], P(('fsdp', 'ctx')), may hold values from -6 to 6
- positions: int32 [16384], P(('fsdp', 'ctx')), may hold values from 0 to 4095, as said below
- attn_gain: bfloat16 [1024], P('fsdp'), may hold values from 0.5 to 1.5
- w_query: bfloat16 [1024, 2048], P('fsdp'), may hold values from -0.1875 to 0.1875
- w_key: bfloat16 [1024, 1024], P('fsdp'), may hold values from -0.1875 to 0.1875
- w_value: bfloat16 [1024, 1024], P('fsdp'), may hold values from -0.1875 to 0.1875
- query_gain: bfloat16 [128], P('fsdp'), may hold values from 0.5 to 1.5
- key_gain: bfloat16 [128], P('fsdp'), may hold values from 0.5 to 1.5
- w_out: bfloat16 [2048, 1024], P('fsdp'), may hold values from -4 to 4
- ffn_gain: bfloat16 [1024], P('fsdp'), may hold values from 0.5 to 1.5
- w_gate: bfloat16 [1024, 3072], P('fsdp'), may hold values from -0.1875 to 0.1875
- w_up: bfloat16 [1024, 3072], P('fsdp'), may hold values from -0.1875 to 0.1875
- w_down: bfloat16 [3072, 1024], P('fsdp'), may hold values from -0.109375 to 0.109375
- cotangent: bfloat16 [16384, 1024], P(('fsdp', 'ctx')), may hold values from -6 to 6
Outputs:
- output: bfloat16 [16384, 1024], P(('fsdp', 'ctx'))
- grad_tokens: float32 [16384, 1024], P(('fsdp', 'ctx'))
- grad_attn_gain: float32 [1024], P('fsdp')
- grad_w_query: float32 [1024, 2048], P('fsdp')
- grad_w_key: float32 [1024, 1024], P('fsdp')
- grad_w_value: float32 [1024, 1024], P('fsdp')
- grad_query_gain: float32 [128], P('fsdp')
- grad_key_gain: float32 [128], P('fsdp')
- grad_w_out: float32 [2048, 1024], P('fsdp')
- grad_ffn_gain: float32 [1024], P('fsdp')
- grad_w_gate: float32 [1024, 3072], P('fsdp')
- grad_w_up: float32 [1024, 3072], P('fsdp')
- grad_w_down: float32 [3072, 1024], P('fsdp')
Inputs may be any that keep to these rules, and one draw needn't show every extreme that they name: Each sequence of 4096 tokens holds a first document of fewer than 128 tokens, possibly empty, and a second one from there to its end; positions count from 0 at each document's start; at least one sequence is a single document.
All inputs are finite; a program needn't handle non-finite values.
Results may differ from a plain program's by a relative error of at most 0.035.
Values may be sent and summed in bfloat16 or wider, within the bound.
No kernel may reach another device: no remote copies, remote signals or barrier semaphores. Data moves between devices by JAX's collectives and lax.ppermute only.
A program may use at most 192 MiB of HBM per device.

v0:
```python
import math

import jax
import jax.numpy as jnp
from jax import lax
from jax.sharding import PartitionSpec as P

EPSILON = 1e-06
THETA = 1000000.0
NEG_BIG = -1e30


def passed_along(shard, axis, by):
    size = lax.axis_size(axis)
    pairs = [(i, i + by) for i in range(size) if 0 <= i + by < size]
    return lax.ppermute(shard, axis, pairs)


def passed_along_2(block, axis, distance):
    devices = range(lax.axis_size(axis))
    route = [((i - distance) % len(devices), i) for i in devices]
    return lax.ppermute(block, axis, route)


def rms_scale(values_in):
    return lax.rsqrt(jnp.mean(values_in * values_in, axis=-1, keepdims=True) + EPSILON)


def rotary_tables(where_at, feature_count):
    half_width = feature_count // 2
    frequency = THETA ** (-(jnp.arange(half_width, dtype=jnp.float32) * 2.0) / feature_count)
    angles = where_at.astype(jnp.float32)[:, None] * frequency[None, :]
    cosine = jnp.concatenate([jnp.cos(angles), jnp.cos(angles)], axis=-1)[:, None, :]
    sine = jnp.concatenate([jnp.sin(angles), jnp.sin(angles)], axis=-1)[:, None, :]
    return (cosine, sine)


def rotate_forward(values_in, cosine, sine):
    half_width = values_in.shape[-1] // 2
    turned = jnp.concatenate([-values_in[..., half_width:], values_in[..., :half_width]], axis=-1)
    return values_in * cosine + turned * sine


def rotate_back(values_in, cosine, sine):
    half_width = values_in.shape[-1] // 2
    shifted = values_in * sine
    turned = jnp.concatenate([shifted[..., half_width:], -shifted[..., :half_width]], axis=-1)
    return values_in * cosine + turned


def norm_back(grad_normed, unit_value, scale_value):
    return scale_value * (
        grad_normed - unit_value * jnp.mean(grad_normed * unit_value, axis=-1, keepdims=True)
    )


def product_back(left, right):
    return lax.dot_general(
        left, right, (((1,), (1,)), ((), ())), preferred_element_type=jnp.float32
    )


def product_over_rows(left, right):
    return lax.dot_general(
        left, right, (((0,), (0,)), ((), ())), preferred_element_type=jnp.float32
    )


def keep_state(carried):
    return carried


def scan_blocks(block_step, carried, pieces):
    length = pieces[0].shape[0]
    block_size = math.gcd(length, 512)
    block_total = length // block_size
    shaped = tuple(
        (member.reshape((block_total, block_size) + member.shape[1:]) for member in pieces)
    )

    def advance(current, block_item):
        block_number, block_pieces = block_item
        return (block_step(current, block_pieces, block_number * block_size), None)

    result, unused = lax.scan(advance, carried, (jnp.arange(block_total, dtype=jnp.int32), shaped))
    return result


def local(
    tokens,
    positions,
    attn_gain,
    w_query,
    w_key,
    w_value,
    query_gain,
    key_gain,
    w_out,
    ffn_gain,
    w_gate,
    w_up,
    w_down,
    cotangent,
):
    gathered = (
        lax.all_gather(attn_gain, "fsdp", axis=0, tiled=True),
        lax.all_gather(w_query, "fsdp", axis=0, tiled=True),
        lax.all_gather(w_key, "fsdp", axis=0, tiled=True),
        lax.all_gather(w_value, "fsdp", axis=0, tiled=True),
        lax.all_gather(query_gain, "fsdp", axis=0, tiled=True),
        lax.all_gather(key_gain, "fsdp", axis=0, tiled=True),
        lax.all_gather(w_out, "fsdp", axis=0, tiled=True),
        lax.all_gather(ffn_gain, "fsdp", axis=0, tiled=True),
        lax.all_gather(w_gate, "fsdp", axis=0, tiled=True),
        lax.all_gather(w_up, "fsdp", axis=0, tiled=True),
        lax.all_gather(w_down, "fsdp", axis=0, tiled=True),
    )
    gain_one = gathered[0].astype(jnp.float32)
    query_full = gathered[1]
    key_full = gathered[2]
    value_full = gathered[3]
    gain_query = gathered[4].astype(jnp.float32)
    gain_key = gathered[5].astype(jnp.float32)
    out_full = gathered[6]
    gain_two = gathered[7].astype(jnp.float32)
    gate_full = gathered[8]
    up_full = gathered[9]
    down_full = gathered[10]
    head_width = gain_query.shape[0]
    heads_q = query_full.shape[1] // head_width
    heads_kv = key_full.shape[1] // head_width
    group_size = heads_q // heads_kv
    row_count = tokens.shape[0]
    score_scale = head_width ** (-0.5)
    row_index = lax.axis_index("ctx") * row_count + jnp.arange(row_count, dtype=jnp.int32)
    lower_bound = row_index - positions
    cosine, sine = rotary_tables(positions, head_width)
    inputs = tokens.astype(jnp.float32)
    scale_one = rms_scale(inputs)
    normal_one = inputs * scale_one
    normed_one = (normal_one * gain_one).astype(jnp.bfloat16)
    query_raw = jnp.dot(normed_one, query_full, preferred_element_type=jnp.float32).reshape(
        row_count, heads_q, head_width
    )
    key_raw = jnp.dot(normed_one, key_full, preferred_element_type=jnp.float32).reshape(
        row_count, heads_kv, head_width
    )
    value_flat = jnp.dot(normed_one, value_full, preferred_element_type=jnp.float32).astype(
        jnp.bfloat16
    )
    scale_q = rms_scale(query_raw)
    unit_q = query_raw * scale_q
    queries = rotate_forward(unit_q * gain_query, cosine, sine).astype(jnp.bfloat16)
    scale_k = rms_scale(key_raw)
    unit_k = key_raw * scale_k
    key_heads = rotate_forward(unit_k * gain_key, cosine, sine).astype(jnp.bfloat16)
    key_flat = key_heads.reshape(row_count, heads_kv * head_width)
    queries_grouped = queries.reshape(row_count, heads_kv, group_size, head_width)

    def visible_pairs(key_index, query_index, query_lower):
        return (key_index[None, :] <= query_index[:, None]) & (
            key_index[None, :] >= query_lower[:, None]
        )

    def forward_step(carried, pieces, first_index):
        block_rows = pieces[0].shape[0]
        key_part = pieces[0].reshape(block_rows, heads_kv, head_width)
        value_part = pieces[1].reshape(block_rows, heads_kv, head_width)

        def forward_compute(current):
            running, denominator, weighted = current
            scores = (
                jnp.einsum(
                    "qkgd,tkd->kgqt", queries_grouped, key_part, preferred_element_type=jnp.float32
                )
                * score_scale
            )
            visible = visible_pairs(
                first_index + jnp.arange(block_rows, dtype=jnp.int32), row_index, lower_bound
            )
            scores = jnp.where(visible, scores, NEG_BIG)
            newest = jnp.maximum(running, jnp.max(scores, axis=-1))
            weights = jnp.where(visible, jnp.exp(scores - newest[..., None]), 0.0)
            factor = jnp.exp(running - newest)
            denominator = denominator * factor + jnp.sum(weights, axis=-1)
            weighted = weighted * factor[..., None] + jnp.einsum(
                "kgqt,tkd->kgqd",
                weights.astype(jnp.bfloat16),
                value_part,
                preferred_element_type=jnp.float32,
            )
            return (newest, denominator, weighted)

        return lax.cond(
            first_index > row_index[row_count - 1], keep_state, forward_compute, carried
        )

    initial = (
        jnp.full((heads_kv, group_size, row_count), NEG_BIG, jnp.float32),
        jnp.zeros((heads_kv, group_size, row_count), jnp.float32),
        jnp.zeros((heads_kv, group_size, row_count, head_width), jnp.float32),
    )
    carried_out = scan_blocks(
        forward_step,
        initial,
        (
            lax.all_gather(key_flat, "ctx", axis=0, tiled=True),
            lax.all_gather(value_flat, "ctx", axis=0, tiled=True),
        ),
    )
    running, denominator, weighted = carried_out
    attention = weighted / denominator[..., None]
    log_total = running + jnp.log(denominator)
    merged = (
        jnp.transpose(attention, (2, 0, 1, 3))
        .reshape(row_count, heads_q * head_width)
        .astype(jnp.bfloat16)
    )
    middle = inputs + jnp.dot(merged, out_full, preferred_element_type=jnp.float32)
    scale_two = rms_scale(middle)
    normal_two = middle * scale_two
    normed_two = (normal_two * gain_two).astype(jnp.bfloat16)
    gate_value = jnp.dot(normed_two, gate_full, preferred_element_type=jnp.float32)
    up_value = jnp.dot(normed_two, up_full, preferred_element_type=jnp.float32)
    gate_sigmoid = jax.nn.sigmoid(gate_value)
    swish = gate_value * gate_sigmoid
    hidden = (swish * up_value).astype(jnp.bfloat16)
    output = (middle + jnp.dot(hidden, down_full, preferred_element_type=jnp.float32)).astype(
        jnp.bfloat16
    )
    grad_output = cotangent.astype(jnp.float32)
    grad_hidden = product_back(cotangent, down_full)
    grad_gate = (
        grad_hidden * up_value * gate_sigmoid * (1.0 + gate_value * (1.0 - gate_sigmoid))
    ).astype(jnp.bfloat16)
    grad_up = (grad_hidden * swish).astype(jnp.bfloat16)
    grad_normed_two = product_back(grad_gate, gate_full) + product_back(grad_up, up_full)
    gain_two_term = jnp.sum(grad_normed_two * normal_two, axis=0)
    grad_middle = grad_output + norm_back(grad_normed_two * gain_two, normal_two, scale_two)
    grad_branch = grad_middle.astype(jnp.bfloat16)
    grad_merged = product_back(grad_branch, out_full).astype(jnp.bfloat16)
    grad_heads = grad_merged.reshape(row_count, heads_kv, group_size, head_width)
    row_delta = jnp.sum(
        jnp.transpose(grad_heads, (1, 2, 0, 3)).astype(jnp.float32) * attention, axis=-1
    )
    grad_start = jnp.zeros((heads_kv, group_size, row_count, head_width), jnp.float32)
    key_start = jnp.zeros((row_count, heads_kv, head_width), jnp.float32)
    cycle_count = lax.axis_size("ctx")

    def cycle_turn(turn, state):
        grad_q_acc, key_block, value_block, grad_k_acc, grad_v_acc = state
        owner = lax.rem(lax.axis_index("ctx") - turn + cycle_count, cycle_count)
        first_index = owner * row_count
        key_part = key_block.reshape(row_count, heads_kv, head_width)
        value_part = value_block.reshape(row_count, heads_kv, head_width)

        def cycle_compute(current):
            grad_q_now, grad_k_now, grad_v_now = current
            scores = (
                jnp.einsum(
                    "qkgd,tkd->kgqt", queries_grouped, key_part, preferred_element_type=jnp.float32
                )
                * score_scale
            )
            visible = visible_pairs(
                first_index + jnp.arange(row_count, dtype=jnp.int32), row_index, lower_bound
            )
            probability = jnp.where(visible, jnp.exp(scores - log_total[..., None]), 0.0)
            grad_prob = jnp.einsum(
                "qkgd,tkd->kgqt", grad_heads, value_part, preferred_element_type=jnp.float32
            )
            grad_scores = (probability * (grad_prob - row_delta[..., None])).astype(jnp.bfloat16)
            grad_q_now = grad_q_now + jnp.einsum(
                "kgqt,tkd->kgqd", grad_scores, key_part, preferred_element_type=jnp.float32
            )
            grad_k_now = grad_k_now + jnp.einsum(
                "kgqt,qkgd->tkd", grad_scores, queries_grouped, preferred_element_type=jnp.float32
            )
            grad_v_now = grad_v_now + jnp.einsum(
                "kgqt,qkgd->tkd",
                probability.astype(jnp.bfloat16),
                grad_heads,
                preferred_element_type=jnp.float32,
            )
            return (grad_q_now, grad_k_now, grad_v_now)

        grad_q_acc, grad_k_acc, grad_v_acc = lax.cond(
            first_index > row_index[row_count - 1],
            keep_state,
            cycle_compute,
            (grad_q_acc, grad_k_acc, grad_v_acc),
        )
        key_block, value_block = passed_along((key_block, value_block), "ctx", 1)
        grad_k_acc, grad_v_acc = (
            passed_along_2(grad_k_acc.astype(jnp.bfloat16), "ctx", 1).astype(grad_k_acc.dtype),
            passed_along_2(grad_v_acc.astype(jnp.bfloat16), "ctx", 1).astype(grad_v_acc.dtype),
        )
        return (grad_q_acc, key_block, value_block, grad_k_acc, grad_v_acc)

    cycle_state = lax.fori_loop(
        0, cycle_count, cycle_turn, (grad_start, key_flat, value_flat, key_start, key_start)
    )
    grad_q = cycle_state[0]
    grad_k = cycle_state[3]
    grad_v = cycle_state[4]
    grad_rot_q = (
        jnp.transpose(grad_q, (2, 0, 1, 3)).reshape(row_count, heads_q, head_width) * score_scale
    )
    grad_scaled_q = rotate_back(grad_rot_q, cosine, sine)
    query_gain_term = jnp.sum(grad_scaled_q * unit_q, axis=(0, 1))
    grad_query = (
        norm_back(grad_scaled_q * gain_query, unit_q, scale_q)
        .reshape(row_count, heads_q * head_width)
        .astype(jnp.bfloat16)
    )
    grad_scaled_k = rotate_back(grad_k * score_scale, cosine, sine)
    key_gain_term = jnp.sum(grad_scaled_k * unit_k, axis=(0, 1))
    grad_key = (
        norm_back(grad_scaled_k * gain_key, unit_k, scale_k)
        .reshape(row_count, heads_kv * head_width)
        .astype(jnp.bfloat16)
    )
    grad_value = grad_v.reshape(row_count, heads_kv * head_width).astype(jnp.bfloat16)
    grad_normed_one = (
        product_back(grad_query, query_full)
        + product_back(grad_key, key_full)
        + product_back(grad_value, value_full)
    )
    gain_one_term = jnp.sum(grad_normed_one * normal_one, axis=0)
    grad_tokens = grad_middle + norm_back(grad_normed_one * gain_one, normal_one, scale_one)
    attention_grads = jnp.concatenate([grad_query, grad_key, grad_value], axis=1)
    feed_grads = jnp.concatenate([grad_gate, grad_up], axis=1)
    first_part = product_over_rows(normed_one, attention_grads)
    second_part = product_over_rows(normed_two, feed_grads)
    input_part = lax.psum_scatter(
        jnp.concatenate([first_part, second_part], axis=1).astype(jnp.bfloat16),
        "fsdp",
        scatter_dimension=0,
        tiled=True,
    )
    output_part = lax.psum_scatter(
        product_over_rows(merged, grad_branch).astype(jnp.bfloat16),
        "fsdp",
        scatter_dimension=0,
        tiled=True,
    )
    down_part = lax.psum_scatter(
        product_over_rows(hidden, cotangent).astype(jnp.bfloat16),
        "fsdp",
        scatter_dimension=0,
        tiled=True,
    )
    gain_parts = (
        lax.psum_scatter(gain_one_term, "fsdp", scatter_dimension=0, tiled=True),
        lax.psum_scatter(query_gain_term, "fsdp", scatter_dimension=0, tiled=True),
        lax.psum_scatter(key_gain_term, "fsdp", scatter_dimension=0, tiled=True),
        lax.psum_scatter(gain_two_term, "fsdp", scatter_dimension=0, tiled=True),
    )
    summed = (
        lax.psum(input_part, "ctx").astype(jnp.float32),
        lax.psum(output_part, "ctx").astype(jnp.float32),
        lax.psum(down_part, "ctx").astype(jnp.float32),
        lax.psum(gain_parts[0].astype(jnp.bfloat16), "ctx").astype(jnp.float32),
        lax.psum(gain_parts[1].astype(jnp.bfloat16), "ctx").astype(jnp.float32),
        lax.psum(gain_parts[2].astype(jnp.bfloat16), "ctx").astype(jnp.float32),
        lax.psum(gain_parts[3].astype(jnp.bfloat16), "ctx").astype(jnp.float32),
    )
    wide = summed[0]
    query_cols = query_full.shape[1]
    key_cols = key_full.shape[1]
    feed_cols = gate_full.shape[1]
    edge_two = query_cols + key_cols
    edge_three = edge_two + key_cols
    edge_four = edge_three + feed_cols
    return (
        output,
        grad_tokens,
        summed[3],
        wide[:, :query_cols],
        wide[:, query_cols:edge_two],
        wide[:, edge_two:edge_three],
        summed[4],
        summed[5],
        summed[1],
        summed[6],
        wide[:, edge_three:edge_four],
        wide[:, edge_four:],
        summed[2],
    )


def solution(mesh):
    in_specs = (
        P(("fsdp", "ctx"), None),
        P(("fsdp", "ctx")),
        P("fsdp"),
        P("fsdp", None),
        P("fsdp", None),
        P("fsdp", None),
        P("fsdp"),
        P("fsdp"),
        P("fsdp", None),
        P("fsdp"),
        P("fsdp", None),
        P("fsdp", None),
        P("fsdp", None),
        P(("fsdp", "ctx"), None),
    )
    out_specs = (
        P(("fsdp", "ctx"), None),
        P(("fsdp", "ctx"), None),
        P("fsdp"),
        P("fsdp", None),
        P("fsdp", None),
        P("fsdp", None),
        P("fsdp"),
        P("fsdp"),
        P("fsdp", None),
        P("fsdp"),
        P("fsdp", None),
        P("fsdp", None),
        P("fsdp", None),
    )
    return jax.shard_map(local, mesh=mesh, in_specs=in_specs, out_specs=out_specs, check_vma=False)
```

profile of v0, /device:TPU:0, one launch (start us, length us, event | category | flops | bytes accessed | tf_op | source)
XLA Modules:
  0.0 2376.0 jit_solution(2991795237788588949)
XLA Ops:
  29.9 11.2 all-gather.12.cloned.1.call-done
  45.7 27.1 %all-gather.18.cloned.1.call-done = bf16[1024,1024]{1,0:T(8,128)(2,1)} async-done(((bf16[256,1024]{1,0:T(8,128)(2,1)}), bf16[1024,1024]{1,0:T(8,128)(2,1)}) %all-gather.18.cloned.1.call-update) | async-done | bytes 2097168 | tf_op jit(solution)/shard_map/all_gather | solution.py:109
  84.7 36.8 %all-gather.16.cloned.1.call-done = bf16[1024,2048]{1,0:T(8,128)(2,1)} async-done(((bf16[256,2048]{1,0:T(8,128)(2,1)}), bf16[1024,2048]{1,0:T(8,128)(2,1)}) %all-gather.16.cloned.1.call-update) | async-done | bytes 4194320 | tf_op jit(solution)/shard_map/all_gather | solution.py:107
  130.8 99.0 %all-gather.14.cloned.1.call-done = bf16[4096,1024]{1,0:T(8,128)(2,1)} async-done(((bf16[128,1024]{1,0:T(8,128)(2,1)}), bf16[4096,1024]{1,0:T(8,128)(2,1)}) %all-gather.14.cloned.1.call-update) | async-done | bytes 8388624 | tf_op jit(solution)/shard_map/all_gather | solution.py:207
  229.8 11.4 copy.144
  241.2 93.9 %all-gather.20.cloned.1.call-done = bf16[4096,1024]{1,0:T(8,128)(2,1)} async-done(((bf16[128,1024]{1,0:T(8,128)(2,1)}), bf16[4096,1024]{1,0:T(8,128)(2,1)}) %all-gather.20.cloned.1.call-update) | async-done | bytes 8388624 | tf_op jit(solution)/shard_map/all_gather | solution.py:208
  335.1 11.6 copy.145
  346.9 32.1 %while.36 = (s32[]{:T(128)}, f32[8,2,128]{2,1,0:T(2,128)S(1)}, f32[8,2,128]{2,1,0:T(2,128)S(1)}, f32[8,2,128,128]{3,2,1,0:T(8,128)S(1)}, s32[8]{0:T(128)S(1)}, /...) while((s32[]{:T(128)}, f32[8,2,128]{2,1,0:T(2,128)S(1)}, ...), condition=%wide.region_8.9_spmd, body=%wide.region_3.8_spmd.sunk | while | flops 551227904 | bytes 21894452 | solution.py:85
  383.8 63.0 %all-gather.24.cloned.1.call-done = bf16[1024,3072]{1,0:T(8,128)(2,1)} async-done(((bf16[256,3072]{1,0:T(8,128)(2,1)}), bf16[1024,3072]{1,0:T(8,128)(2,1)}) %all-gather.24.cloned.1.call-update) | async-done | bytes 6291472 | tf_op jit(solution)/shard_map/all_gather | solution.py:114
  451.7 61.6 %all-gather.26.cloned.1.call-done = bf16[1024,3072]{1,0:T(8,128)(2,1)} async-done(((bf16[256,3072]{1,0:T(8,128)(2,1)}), bf16[1024,3072]{1,0:T(8,128)(2,1)}) %all-gather.26.cloned.1.call-update) | async-done | bytes 6291472 | tf_op jit(solution)/shard_map/all_gather | solution.py:115
  518.2 61.6 %all-gather.28.cloned.1.call-done = bf16[3072,1024]{1,0:T(8,128)(2,1)} async-done(((bf16[768,1024]{1,0:T(8,128)(2,1)}), bf16[3072,1024]{1,0:T(8,128)(2,1)}) %all-gather.28.cloned.1.call-update) | async-done | bytes 6291472 | tf_op jit(solution)/shard_map/all_gather | solution.py:116
  621.1 1062.9 %while.37 = (s32[]{:T(128)}, f32[8,2,128,128]{3,2,1,0:T(8,128)S(1)}, bf16[128,1024]{1,0:T(8,128)(2,1)}, bf16[128,1024]{1,0:T(8,128)(2,1)S(1)}, f32[128,8,128]{2,...) while((s32[]{:T(128)}, ...), condition=%wide.region_15.16_spmd.clone, body=%wide.region_12.15_spmd.clone.sunk | while | flops 338739328 | bytes 23382648 | solution.py:300
  651.6 10.4 collective-permute-done.3
  698.1 10.2 collective-permute-done.3
  714.6 10.8 collective-permute-done.1
  735.1 9.2 collective-permute-start.3
  817.9 10.1 collective-permute-start.1
  884.9 8.2 collective-permute-start.1
  921.2 8.2 collective-permute-start.1
  947.9 8.8 collective-permute-start
  956.7 8.2 collective-permute-start.1
  987.5 12.1 collective-permute-start.1
  1111.1 8.2 collective-permute-start.1
  1143.8 8.2 collective-permute-start.1
  1175.7 8.2 collective-permute-start.1
  1206.7 8.2 collective-permute-start.1
  1597.6 9.6 collective-permute-start.1
  1709.9 12.8 pad_maximum_fusion
  1722.8 214.1 %reduce-scatter.4.cloned.1.call-done = bf16[256,10240]{1,0:T(8,128)(2,1)} async-done(((bf16[1024,10240]{1,0:T(8,128)(2,1)}), bf16[256,10240]{1,0:T(8,128)(2,1)}) %reduce-scatter.4.cloned.1.call-update) | async-done | bytes 5242896 | tf_op jit(solution)/shard_map/reduce_scatter | solution.py:335
  1945.0 10.7 all-reduce.6
  1956.1 97.5 %all-reduce.7 = (bf16[256]{0:T(256)(128)(2,1)S(1)}, bf16[32]{0:T(256)(128)(2,1)S(1)}, bf16[32]{0:T(256)(128)(2,1)S(1)}, bf16[256]{0:T(256)(128)(2,1)S(1)}) all-reduce(bf16[256]{0:T(256)(128)(2,1)S(1)} %dynamic-slice.15, bf16[32]{0:T(256)(128)(2,1)S(1)} %dynamic-slice.17, ...), channel_id=1, replica_groups=mesh['fsdp'=4,'ctx'=32] {'ctx'}, use_global_device_ids=true, to_apply=%region_21.22 | all-reduce | flops 576 | bytes 2304 | tf_op jit(solution)/shard_map/psum | solution.py:363
  2061.3 294.8 %all-reduce.12.cloned.1.call-done = (bf16[256,10240]{1,0:T(8,128)(2,1)}, bf16[512,1024]{1,0:T(8,128)(2,1)}, bf16[768,1024]{1,0:T(8,128)(2,1)}) async-done(((bf16[256,10240]{1,0:T(8,128)(2,1)}, bf16[512,1024]{1,0:T(8,128)(2,1)}, bf16[768,1024]{1,0:T(8,128)(2,1)}), (bf16[256,10240]{1,0:T(8,128)(2,1)}, bf16[512,1024]{1,0:T(8,128)(2,1)}, bf16[768,1024]{1,0:T(8,128)(2,1)})) %all-reduce.12.cloned.1.call-update) | async-done | bytes 7864336 | tf_op jit(solution)/shard_map/psum | solution.py:360
  (837 shorter events, 1089.6 us)
Async XLA Ops:
  7.2 34.0 %all-gather.12.cloned.1.call-start = ((), (), s32[]{:S(2)}) async-start(), calls=%async_computation.3 | async-start | bytes 2621440 | tf_op jit(solution)/shard_map/all_gather | solution.py:108
  7.9 64.9 %all-gather.18.cloned.1.call-start = ((), (), s32[]{:S(2)}) async-start(), calls=%async_computation.6 | async-start | bytes 2621440 | tf_op jit(solution)/shard_map/all_gather | solution.py:109
  8.7 112.9 %all-gather.16.cloned.1.call-start = ((), (), s32[]{:S(2)}) async-start(), calls=%async_computation.5 | async-start | bytes 5242880 | tf_op jit(solution)/shard_map/all_gather | solution.py:107
  9.4 220.4 %all-gather.14.cloned.1.call-start = ((), (), s32[]{:S(2)}) async-start(), calls=%async_computation.4 | async-start | bytes 8650752 | tf_op jit(solution)/shard_map/all_gather | solution.py:207
  45.7 289.5 %all-gather.20.cloned.1.call-start = ((), (), s32[]{:S(2)}) async-start(), calls=%async_computation.7 | async-start | bytes 8650752 | tf_op jit(solution)/shard_map/all_gather | solution.py:208
  75.7 304.9 %all-gather.22.cloned.1.call-start = ((), (), s32[]{:S(2)}) async-start(), calls=%async_computation.8 | async-start | bytes 5242880 | tf_op jit(solution)/shard_map/all_gather | solution.py:112
  76.2 370.5 %all-gather.24.cloned.1.call-start = ((), (), s32[]{:S(2)}) async-start(), calls=%async_computation.9 | async-start | bytes 7864320 | tf_op jit(solution)/shard_map/all_gather | solution.py:114
  77.0 436.3 %all-gather.26.cloned.1.call-start = ((), (), s32[]{:S(2)}) async-start(), calls=%async_computation.10 | async-start | bytes 7864320 | tf_op jit(solution)/shard_map/all_gather | solution.py:115
  77.7 502.1 %all-gather.28.cloned.1.call-start = ((), (), s32[]{:S(2)}) async-start(), calls=%async_computation.11 | async-start | bytes 7864320 | tf_op jit(solution)/shard_map/all_gather | solution.py:116
  78.5 1644.3 %reduce-scatter.6.cloned.1.call-start = ((), (), s32[]{:S(2)}) async-start(), calls=%async_computation.13 | async-start | bytes 5242880 | tf_op jit(solution)/shard_map/reduce_scatter | solution.py:341
  599.1 1123.7 %reduce-scatter.8.cloned.1.call-start = ((), (), s32[]{:S(2)}) async-start(), calls=%async_computation.14 | async-start | bytes 7864320 | tf_op jit(solution)/shard_map/reduce_scatter | solution.py:347
  620.2 1316.7 %reduce-scatter.4.cloned.1.call-start = ((), (), s32[]{:S(2)}) async-start(), calls=%async_computation.12 | async-start | bytes 26214400 | tf_op jit(solution)/shard_map/reduce_scatter | solution.py:335
  632.6 29.3 %collective-permute-start.3 = (bf16[128,8,128]{2,0,1:T(8,128)(2,1)S(1)}, bf16[128,8,128]{2,0,1:T(8,128)(2,1)S(1)}, u32[]{:S(2)}, u32[]{:S(2)}) collective-permute-start(bf16[128,8,128]{2,0,1:T(8,128)(2,1)S(1)} %convert_element_type.309), channel_id=1, source_target_pairs={{31,0},{0,1},{1,2},{2,3},{3,4},{4,5},{5,6},{6,7},{7,8},{8,9},{9,10... | collective-permute-start | bytes 786440 | tf_op jit(solution)/shard_map/while/body/eval_jaxpr/ppermute | solution.py:22
  634.5 28.4 %collective-permute-start = (bf16[128,1024]{1,0:T(8,128)(2,1)}, bf16[128,1024]{1,0:T(8,128)(2,1)}, u32[]{:S(2)}, u32[]{:S(2)}) collective-permute-start(bf16[128,1024]{1,0:T(8,128)(2,1)} %copy.262), channel_id=1, source_target_pairs={{0,1},{1,2},{2,3},{3,4},{4,5},{5,6},{6,7},{7,8},{8,9},{9,10},{10,1... | collective-permute-start | bytes 786440 | tf_op jit(solution)/shard_map/while/body/eval_jaxpr/ppermute | solution.py:16
  639.7 25.8 %collective-permute-start.1 = (bf16[128,1024]{1,0:T(8,128)(2,1)S(1)}, bf16[128,1024]{1,0:T(8,128)(2,1)S(1)}, u32[]{:S(2)}, u32[]{:S(2)}) collective-permute-start(bf16[128,1024]{1,0:T(8,128)(2,1)S(1)} %copy.263), channel_id=1, source_target_pairs={{0,1},{1,2},{2,3},{3,4},{4,5},{5,6},{6,7},{7,8},{8,9},{9,10},{10,1... | collective-permute-start | bytes 786440 | tf_op jit(solution)/shard_map/while/body/eval_jaxpr/ppermute | solution.py:16
  671.4 25.9 %collective-permute-start.2 = (bf16[128,8,128]{2,0,1:T(8,128)(2,1)}, bf16[128,8,128]{2,0,1:T(8,128)(2,1)S(1)}, u32[]{:S(2)}, u32[]{:S(2)}) collective-permute-start(bf16[128,8,128]{2,0,1:T(8,128)(2,1)} %convert_element_type.307), channel_id=1, source_target_pairs={{31,0},{0,1},{1,2},{2,3},{3,4},{4,5},{5,6},{6,7},{7,8},{8,9},{9,10... | collective-permute-start | bytes 786440 | tf_op jit(solution)/shard_map/while/body/eval_jaxpr/ppermute | solution.py:22
  679.6 28.7 %collective-permute-start.3 = (bf16[128,8,128]{2,0,1:T(8,128)(2,1)S(1)}, bf16[128,8,128]{2,0,1:T(8,128)(2,1)S(1)}, u32[]{:S(2)}, u32[]{:S(2)}) collective-permute-start(bf16[128,8,128]{2,0,1:T(8,128)(2,1)S(1)} %convert_element_type.309), channel_id=1, source_target_pairs={{31,0},{0,1},{1,2},{2,3},{3,4},{4,5},{5,6},{6,7},{7,8},{8,9},{9,10... | collective-permute-start | bytes 786440 | tf_op jit(solution)/shard_map/while/body/eval_jaxpr/ppermute | solution.py:22
  683.6 31.0 %collective-permute-start = (bf16[128,1024]{1,0:T(8,128)(2,1)}, bf16[128,1024]{1,0:T(8,128)(2,1)}, u32[]{:S(2)}, u32[]{:S(2)}) collective-permute-start(bf16[128,1024]{1,0:T(8,128)(2,1)} %copy.262), channel_id=1, source_target_pairs={{0,1},{1,2},{2,3},{3,4},{4,5},{5,6},{6,7},{7,8},{8,9},{9,10},{10,1... | collective-permute-start | bytes 786440 | tf_op jit(solution)/shard_map/while/body/eval_jaxpr/ppermute | solution.py:16
  686.9 38.6 %collective-permute-start.1 = (bf16[128,1024]{1,0:T(8,128)(2,1)S(1)}, bf16[128,1024]{1,0:T(8,128)(2,1)S(1)}, u32[]{:S(2)}, u32[]{:S(2)}) collective-permute-start(bf16[128,1024]{1,0:T(8,128)(2,1)S(1)} %copy.263), channel_id=1, source_target_pairs={{0,1},{1,2},{2,3},{3,4},{4,5},{5,6},{6,7},{7,8},{8,9},{9,10},{10,1... | collective-permute-start | bytes 786440 | tf_op jit(solution)/shard_map/while/body/eval_jaxpr/ppermute | solution.py:16
  802.1 25.9 %collective-permute-start.2 = (bf16[128,8,128]{2,0,1:T(8,128)(2,1)}, bf16[128,8,128]{2,0,1:T(8,128)(2,1)S(1)}, u32[]{:S(2)}, u32[]{:S(2)}) collective-permute-start(bf16[128,8,128]{2,0,1:T(8,128)(2,1)} %convert_element_type.307), channel_id=1, source_target_pairs={{31,0},{0,1},{1,2},{2,3},{3,4},{4,5},{5,6},{6,7},{7,8},{8,9},{9,10... | collective-permute-start | bytes 786440 | tf_op jit(solution)/shard_map/while/body/eval_jaxpr/ppermute | solution.py:22
  837.5 25.5 %collective-permute-start.2 = (bf16[128,8,128]{2,0,1:T(8,128)(2,1)}, bf16[128,8,128]{2,0,1:T(8,128)(2,1)S(1)}, u32[]{:S(2)}, u32[]{:S(2)}) collective-permute-start(bf16[128,8,128]{2,0,1:T(8,128)(2,1)} %convert_element_type.307), channel_id=1, source_target_pairs={{31,0},{0,1},{1,2},{2,3},{3,4},{4,5},{5,6},{6,7},{7,8},{8,9},{9,10... | collective-permute-start | bytes 786440 | tf_op jit(solution)/shard_map/while/body/eval_jaxpr/ppermute | solution.py:22
  841.6 24.3 %collective-permute-start.3 = (bf16[128,8,128]{2,0,1:T(8,128)(2,1)S(1)}, bf16[128,8,128]{2,0,1:T(8,128)(2,1)S(1)}, u32[]{:S(2)}, u32[]{:S(2)}) collective-permute-start(bf16[128,8,128]{2,0,1:T(8,128)(2,1)S(1)} %convert_element_type.309), channel_id=1, source_target_pairs={{31,0},{0,1},{1,2},{2,3},{3,4},{4,5},{5,6},{6,7},{7,8},{8,9},{9,10... | collective-permute-start | bytes 786440 | tf_op jit(solution)/shard_map/while/body/eval_jaxpr/ppermute | solution.py:22
  872.4 25.2 %collective-permute-start.2 = (bf16[128,8,128]{2,0,1:T(8,128)(2,1)}, bf16[128,8,128]{2,0,1:T(8,128)(2,1)S(1)}, u32[]{:S(2)}, u32[]{:S(2)}) collective-permute-start(bf16[128,8,128]{2,0,1:T(8,128)(2,1)} %convert_element_type.307), channel_id=1, source_target_pairs={{31,0},{0,1},{1,2},{2,3},{3,4},{4,5},{5,6},{6,7},{7,8},{8,9},{9,10... | collective-permute-start | bytes 786440 | tf_op jit(solution)/shard_map/while/body/eval_jaxpr/ppermute | solution.py:22
  873.7 26.7 %collective-permute-start.3 = (bf16[128,8,128]{2,0,1:T(8,128)(2,1)S(1)}, bf16[128,8,128]{2,0,1:T(8,128)(2,1)S(1)}, u32[]{:S(2)}, u32[]{:S(2)}) collective-permute-start(bf16[128,8,128]{2,0,1:T(8,128)(2,1)S(1)} %convert_element_type.309), channel_id=1, source_target_pairs={{31,0},{0,1},{1,2},{2,3},{3,4},{4,5},{5,6},{6,7},{7,8},{8,9},{9,10... | collective-permute-start | bytes 786440 | tf_op jit(solution)/shard_map/while/body/eval_jaxpr/ppermute | solution.py:22
  906.9 24.4 %collective-permute-start.2 = (bf16[128,8,128]{2,0,1:T(8,128)(2,1)}, bf16[128,8,128]{2,0,1:T(8,128)(2,1)S(1)}, u32[]{:S(2)}, u32[]{:S(2)}) collective-permute-start(bf16[128,8,128]{2,0,1:T(8,128)(2,1)} %convert_element_type.307), channel_id=1, source_target_pairs={{31,0},{0,1},{1,2},{2,3},{3,4},{4,5},{5,6},{6,7},{7,8},{8,9},{9,10... | collective-permute-start | bytes 786440 | tf_op jit(solution)/shard_map/while/body/eval_jaxpr/ppermute | solution.py:22
  906.9 27.1 %collective-permute-start.3 = (bf16[128,8,128]{2,0,1:T(8,128)(2,1)S(1)}, bf16[128,8,128]{2,0,1:T(8,128)(2,1)S(1)}, u32[]{:S(2)}, u32[]{:S(2)}) collective-permute-start(bf16[128,8,128]{2,0,1:T(8,128)(2,1)S(1)} %convert_element_type.309), channel_id=1, source_target_pairs={{31,0},{0,1},{1,2},{2,3},{3,4},{4,5},{5,6},{6,7},{7,8},{8,9},{9,10... | collective-permute-start | bytes 786440 | tf_op jit(solution)/shard_map/while/body/eval_jaxpr/ppermute | solution.py:22
  940.6 24.4 %collective-permute-start.2 = (bf16[128,8,128]{2,0,1:T(8,128)(2,1)}, bf16[128,8,128]{2,0,1:T(8,128)(2,1)S(1)}, u32[]{:S(2)}, u32[]{:S(2)}) collective-permute-start(bf16[128,8,128]{2,0,1:T(8,128)(2,1)} %convert_element_type.307), channel_id=1, source_target_pairs={{31,0},{0,1},{1,2},{2,3},{3,4},{4,5},{5,6},{6,7},{7,8},{8,9},{9,10... | collective-permute-start | bytes 786440 | tf_op jit(solution)/shard_map/while/body/eval_jaxpr/ppermute | solution.py:22
  974.4 25.2 %collective-permute-start.2 = (bf16[128,8,128]{2,0,1:T(8,128)(2,1)}, bf16[128,8,128]{2,0,1:T(8,128)(2,1)S(1)}, u32[]{:S(2)}, u32[]{:S(2)}) collective-permute-start(bf16[128,8,128]{2,0,1:T(8,128)(2,1)} %convert_element_type.307), channel_id=1, source_target_pairs={{31,0},{0,1},{1,2},{2,3},{3,4},{4,5},{5,6},{6,7},{7,8},{8,9},{9,10... | collective-permute-start | bytes 786440 | tf_op jit(solution)/shard_map/while/body/eval_jaxpr/ppermute | solution.py:22
  1581.4 25.8 %collective-permute-start.2 = (bf16[128,8,128]{2,0,1:T(8,128)(2,1)}, bf16[128,8,128]{2,0,1:T(8,128)(2,1)S(1)}, u32[]{:S(2)}, u32[]{:S(2)}) collective-permute-start(bf16[128,8,128]{2,0,1:T(8,128)(2,1)} %convert_element_type.307), channel_id=1, source_target_pairs={{31,0},{0,1},{1,2},{2,3},{3,4},{4,5},{5,6},{6,7},{7,8},{8,9},{9,10... | collective-permute-start | bytes 786440 | tf_op jit(solution)/shard_map/while/body/eval_jaxpr/ppermute | solution.py:22
  1653.0 27.2 %collective-permute-start.2 = (bf16[128,8,128]{2,0,1:T(8,128)(2,1)}, bf16[128,8,128]{2,0,1:T(8,128)(2,1)S(1)}, u32[]{:S(2)}, u32[]{:S(2)}) collective-permute-start(bf16[128,8,128]{2,0,1:T(8,128)(2,1)} %convert_element_type.307), channel_id=1, source_target_pairs={{31,0},{0,1},{1,2},{2,3},{3,4},{4,5},{5,6},{6,7},{7,8},{8,9},{9,10... | collective-permute-start | bytes 786440 | tf_op jit(solution)/shard_map/while/body/eval_jaxpr/ppermute | solution.py:22
  1657.1 26.0 %collective-permute-start.3 = (bf16[128,8,128]{2,0,1:T(8,128)(2,1)S(1)}, bf16[128,8,128]{2,0,1:T(8,128)(2,1)S(1)}, u32[]{:S(2)}, u32[]{:S(2)}) collective-permute-start(bf16[128,8,128]{2,0,1:T(8,128)(2,1)S(1)} %convert_element_type.309), channel_id=1, source_target_pairs={{31,0},{0,1},{1,2},{2,3},{3,4},{4,5},{5,6},{6,7},{7,8},{8,9},{9,10... | collective-permute-start | bytes 786440 | tf_op jit(solution)/shard_map/while/body/eval_jaxpr/ppermute | solution.py:22
  1722.7 633.4 %all-reduce.12.cloned.1.call-start = ((), (), s32[]{:S(2)}) async-start(), calls=%async_computation.15 | async-start | bytes 15728640 | tf_op jit(solution)/shard_map/psum | solution.py:360
  (163 other events, 4478.6 us)
Sparse Core Ops, SparseCore 0:
  9.7 31.4 all-gather.11
  42.8 29.9 all-gather.17
  74.5 47.0 all-gather.15
  124.5 105.2 all-gather.13
  233.3 101.7 all-gather.19
  336.6 43.9 all-gather.21
  382.3 64.4 all-gather.23
  448.4 64.8 all-gather.25
  515.0 64.8 all-gather.27
  599.2 57.2 reduce-scatter.5
  659.1 93.0 reduce-scatter.7
  1722.8 214.0 reduce-scatter.3
  1939.7 416.3 all-reduce.11
where the time goes:
time: 2390 us; the launch traced here: 2380 us
  waiting for transfers between devices  1140 us (48%)
  starting transfers between devices  653 us (27%)
  local copies, waits for them, and re-layouts  171 us (7%)
  other arithmetic  159 us (7%)
  blocking collectives  126 us (5%)
  matrix products  75.7 us (3%)
  loops' own time  34.5 us (1%)
    ppermute x64, starting transfers between devices, passed_along(): return lax.ppermute(shard, axis, pairs)  380 us
    psum x1, waiting for transfers between devices, local(): lax.psum(input_part, 'ctx').astype(jnp.float32)  295 us
    ppermute x64, starting transfers between devices, passed_along_2(): return lax.ppermute(block, axis, route)  272 us
    reduce_scatter x1, waiting for transfers between devices, local(): lax.psum_scatter(jnp.concatenate([first_part, second_part], axis=1).astyp...  214 us
    all_gather x1, waiting for transfers between devices, local(): lax.all_gather(key_flat, 'ctx', axis=0, tiled=True)  99 us
    psum x1, blocking collectives, local(): lax.psum(gain_parts[0].astype(jnp.bfloat16), 'ctx').astype(jnp.float32)  97.5 us
    all_gather x1, waiting for transfers between devices, local(): lax.all_gather(value_flat, 'ctx', axis=0, tiled=True)  93.9 us
    ppermute x64, waiting for transfers between devices, passed_along(): return lax.ppermute(shard, axis, pairs)  85.5 us
  transfers between devices with their start and end apart: 141, of which 75 were waited for; matrix products, arithmetic and copies ran while one was open for 16% of the time, Pallas kernels for 0%

commit v1 on v0

v1 whole, which is shorter than its diff:
```python
import jax
import jax.numpy as jnp
from jax import lax
from jax.experimental import pallas as pl
from jax.experimental.pallas import tpu as pltpu
from jax.sharding import Mesh
from jax.sharding import PartitionSpec as P

EPSILON = 1e-06
THETA = 1000000.0
HEAD = 128
ROWS = 128
CHUNK = 512
SCORE_SCALE = HEAD ** (-0.5)
LOG2_E = 1.4426950408889634
EXP_SCALE = SCORE_SCALE * LOG2_E
LOW = jnp.bfloat16
F32 = jnp.float32


def x_shift(value, step):
    pairs = []
    for x in range(4):
        to = (x + step) % 4
        pairs.append(((x % 2) * 2 + x // 2, (to % 2) * 2 + to // 2))
    return lax.ppermute(value, ("xl", "xh"), pairs)


def shift(value, axis, step):
    if axis == "x":
        return x_shift(value, step)
    return lax.ppermute(value, axis, [(i, (i + step) % 4) for i in range(4)])


def core_swap(value):
    return lax.ppermute(value, "co", [(0, 1), (1, 0)])


def place_on(axis):
    if axis == "x":
        return lax.axis_index("xh") * 2 + lax.axis_index("xl")
    return lax.axis_index(axis)


def pick(value, index, dim):
    return lax.dynamic_index_in_dim(value, index, dim, keepdims=False)


def reduce_over(value, axis, dim):
    me = place_on(axis)
    total = pick(value, me, dim).astype(F32)
    for step in (1, 3, 2):
        total = total + shift(pick(value, (me + step) % 4, dim), axis, step).astype(F32)
    return total.astype(LOW)


def gather_over(value, axis, dim, dtype=LOW):
    me = place_on(axis)
    shape = value.shape[:dim] + (4,) + value.shape[dim:]
    out = jnp.zeros(shape, dtype)
    out = lax.dynamic_update_index_in_dim(out, value.astype(dtype), me, dim)
    for step in (1, 3, 2):
        got = shift(value, axis, step).astype(dtype)
        out = lax.dynamic_update_index_in_dim(out, got, (me - step) % 4, dim)
    return out


def sum_everywhere(grads):
    cols = grads.shape[-1]
    half = cols // 2
    parts = grads.reshape(2, 4, 4, 16, cols)
    first, second = parts[..., :half], parts[..., half:]
    first = reduce_over(first, "y", 1)
    second = reduce_over(second, "z", 2)
    first = reduce_over(first, "z", 1)
    second = reduce_over(second, "y", 1)
    both = jnp.stack([first, second], axis=0)
    mine = reduce_over(both.reshape(4, 16, half), "x", 0)
    xh = lax.axis_index("xh")
    other = lax.ppermute(mine, "xh", [(0, 1), (1, 0)])
    first = jnp.where(xh == 0, mine, other)
    second = jnp.where(xh == 0, other, mine)
    first = gather_over(first, "z", 0)
    second = gather_over(second, "y", 0)
    first = gather_over(first, "y", 0, F32).reshape(256, half)
    second = gather_over(second, "z", 1, F32).reshape(256, half)
    return first, second


def gather_weight(shard):
    rows = shard.shape[0]
    half = rows // 2
    up = x_shift(shard[:half], 1)
    down = x_shift(shard[half:], -1)
    own_swapped = core_swap(shard)
    up_swapped = core_swap(up)
    down_swapped = core_swap(down)
    xl = lax.axis_index("xl")
    co = lax.axis_index("co")
    out = jnp.zeros((rows * 4, shard.shape[1]), shard.dtype)
    here = (xl * 2 + co) * rows
    there = ((1 - xl) * 2 + co) * rows
    here_other = (xl * 2 + 1 - co) * rows
    there_other = ((1 - xl) * 2 + 1 - co) * rows
    for piece, at in (
        (shard, here),
        (up, there),
        (down, there + half),
        (own_swapped, here_other),
        (up_swapped, there_other),
        (down_swapped, there_other + half),
    ):
        out = lax.dynamic_update_slice_in_dim(out, piece, at, 0)
    return out, (up, down)


def visible(first_key, query_block, start):
    key = first_key + lax.broadcasted_iota(jnp.int32, (CHUNK, 2 * ROWS), 0)
    query = query_block * ROWS + (lax.broadcasted_iota(jnp.int32, (CHUNK, 2 * ROWS), 1) & (ROWS - 1))
    return (key <= query) & ((key >= start) | (query < start))


def dot_t(left, right):
    return lax.dot_general(left, right, (((1,), (1,)), ((), ())), preferred_element_type=F32)


def dot_n(left, right):
    return lax.dot_general(left, right, (((1,), (0,)), ((), ())), preferred_element_type=F32)


def block_of(info):
    i = pl.program_id(0)
    return (i // 2) * 8 + info[1] * 2 + i % 2


def forward_kernel(info, q_ref, k_ref, vt_ref, o_ref, l_ref):
    block = block_of(info)
    start = info[0]
    q = q_ref[0]
    last = block // (CHUNK // ROWS)

    def step(c, carry, masked):
        total, mixed = carry
        keys = k_ref[pl.ds(pl.multiple_of(c * CHUNK, CHUNK), CHUNK), :]
        p = jnp.exp2(dot_t(keys, q) * EXP_SCALE)
        if masked:
            p = jnp.where(visible(c * CHUNK, block, start), p, 0.0)
        total = total + jnp.sum(p.reshape(CHUNK // 8, 8, 2 * ROWS), axis=0)
        mixed = mixed + dot_n(vt_ref[c], p.astype(LOW))
        return total, mixed

    carry = (jnp.zeros((8, 2 * ROWS), F32), jnp.zeros((HEAD, 2 * ROWS), F32))
    carry = step(last, carry, True)
    carry = lax.fori_loop(0, jnp.minimum(last, 1), lambda c, x: step(c, x, True), carry)
    carry = lax.fori_loop(1, last, lambda c, x: step(c, x, False), carry)
    total = jnp.sum(carry[0], axis=0, keepdims=True)
    o_ref[0] = carry[1] / total
    l_ref[0] = jnp.log2(total)


def backward_kernel(
    info, q_ref, do_ref, ot_ref, l_ref, k_ref, kt_ref, v_ref, dq_ref, dkv_ref, dk_acc, dv_acc
):
    i = pl.program_id(0)
    block = block_of(info)
    start = info[0]
    q = q_ref[0]
    do = do_ref[0]
    last = block // (CHUNK // ROWS)

    @pl.when(i == 0)
    def _():
        dk_acc[...] = jnp.zeros_like(dk_acc)
        dv_acc[...] = jnp.zeros_like(dv_acc)

    delta = jnp.sum(do.astype(F32).T * ot_ref[0], axis=0, keepdims=True)
    logs = l_ref[0]

    def step(c, dqt, masked):
        at = pl.ds(pl.multiple_of(c * CHUNK, CHUNK), CHUNK)
        p = jnp.exp2(dot_t(k_ref[at, :], q) * EXP_SCALE - logs)
        if masked:
            p = jnp.where(visible(c * CHUNK, block, start), p, 0.0)
        dp = dot_t(v_ref[at, :], do)
        ds = (p * (dp - delta)).astype(LOW)
        dv_acc[at, :] += dot_n(p.astype(LOW), do)
        dk_acc[at, :] += dot_n(ds, q)
        return dqt + dot_n(kt_ref[c], ds)

    dqt = step(last, jnp.zeros((HEAD, 2 * ROWS), F32), True)
    dqt = lax.fori_loop(0, jnp.minimum(last, 1), lambda c, x: step(c, x, True), dqt)
    dqt = lax.fori_loop(1, last, lambda c, x: step(c, x, False), dqt)
    dq_ref[0] = (dqt * SCORE_SCALE).T.astype(LOW)

    @pl.when(i == pl.num_programs(0) - 1)
    def _():
        dkv_ref[:, :HEAD] = (dk_acc[...] * SCORE_SCALE).astype(LOW)
        dkv_ref[:, HEAD:] = dv_acc[...].astype(LOW)


def whole(shape):
    return pl.BlockSpec(shape, lambda i: (0,) * len(shape))


def per_block(shape):
    return pl.BlockSpec((1,) + shape, lambda i: (i,) + (0,) * len(shape))


def smem():
    return pl.BlockSpec(memory_space=pltpu.SMEM)


def attention_forward(info, q, k, vt):
    length = k.shape[0]
    return pl.pallas_call(
        forward_kernel,
        grid=(8,),
        in_specs=[
            smem(),
            per_block((2 * ROWS, HEAD)),
            whole((length, HEAD)),
            whole((length // CHUNK, HEAD, CHUNK)),
        ],
        out_specs=[per_block((HEAD, 2 * ROWS)), per_block((1, 2 * ROWS))],
        out_shape=[
            jax.ShapeDtypeStruct((8, HEAD, 2 * ROWS), F32),
            jax.ShapeDtypeStruct((8, 1, 2 * ROWS), F32),
        ],
        compiler_params=pltpu.CompilerParams(vmem_limit_bytes=24 * 2**20),
        cost_estimate=pl.CostEstimate(
            flops=3 * 10**9, bytes_accessed=5 * 2**20, transcendentals=5 * 10**6
        ),
        name="attention_forward",
    )(info, q, k, vt)


def attention_backward(info, q, do, ot, logs, k, kt, v):
    length = k.shape[0]
    return pl.pallas_call(
        backward_kernel,
        grid=(8,),
        in_specs=[
            smem(),
            per_block((2 * ROWS, HEAD)),
            per_block((2 * ROWS, HEAD)),
            per_block((HEAD, 2 * ROWS)),
            per_block((1, 2 * ROWS)),
            whole((length, HEAD)),
            whole((length // CHUNK, HEAD, CHUNK)),
            whole((length, HEAD)),
        ],
        out_specs=[per_block((2 * ROWS, HEAD)), whole((length, 2 * HEAD))],
        out_shape=[
            jax.ShapeDtypeStruct((8, 2 * ROWS, HEAD), LOW),
            jax.ShapeDtypeStruct((length, 2 * HEAD), LOW),
        ],
        scratch_shapes=[pltpu.VMEM((length, HEAD), F32), pltpu.VMEM((length, HEAD), F32)],
        compiler_params=pltpu.CompilerParams(vmem_limit_bytes=32 * 2**20),
        cost_estimate=pl.CostEstimate(
            flops=8 * 10**9, bytes_accessed=10 * 2**20, transcendentals=5 * 10**6
        ),
        name="attention_backward",
    )(info, q, do, ot, logs, k, kt, v)


def rms_scale(values_in):
    return lax.rsqrt(jnp.mean(values_in * values_in, axis=-1, keepdims=True) + EPSILON)


def rotary_tables(where_at):
    half = HEAD // 2
    frequency = THETA ** (-(jnp.arange(half, dtype=F32) * 2.0) / HEAD)
    angles = where_at.astype(F32)[:, None] * frequency[None, :]
    cosine, sine = jnp.cos(angles), jnp.sin(angles)
    cosine = jnp.concatenate([cosine, cosine], axis=-1)[:, None, :]
    sine = jnp.concatenate([sine, sine], axis=-1)[:, None, :]
    return cosine, sine


def rotate_forward(u, cosine, sine):
    half = HEAD // 2
    turned = jnp.concatenate([-u[..., half:], u[..., :half]], axis=-1)
    return u * cosine + turned * sine


def rotate_back(w, cosine, sine):
    half = HEAD // 2
    shifted = w * sine
    turned = jnp.concatenate([shifted[..., half:], -shifted[..., :half]], axis=-1)
    return w * cosine + turned


def norm_back(grad, unit, scale):
    return scale * (grad - unit * jnp.mean(grad * unit, axis=-1, keepdims=True))


def over_rows(left, right):
    return lax.dot_general(left, right, (((0,), (0,)), ((), ())), preferred_element_type=F32)


def dot(left, right):
    return jnp.dot(left, right, preferred_element_type=F32)


def exchange_heads(value):
    return lax.all_to_all(value, ("z", "xh"), split_axis=0, concat_axis=0, tiled=True)


def exchange_y(value):
    return lax.all_to_all(value, "y", split_axis=0, concat_axis=0, tiled=True)


def column_groups(value, co):
    rows, cols = value.shape
    split = value.reshape(rows, 2, 2, cols // 4)
    mine = pick(split, co, 2)
    other = pick(split, 1 - co, 2)
    return mine.reshape(rows, cols // 2), other.reshape(rows, cols // 2)


def both_cores(value):
    return jnp.concatenate([value, core_swap(value)], axis=0)


def both_cores_columns(value, co):
    mine, other = column_groups(value, co)
    return jnp.concatenate([mine, core_swap(other)], axis=0)


def local(
    tokens,
    positions,
    attn_gain,
    w_query,
    w_key,
    w_value,
    query_gain,
    key_gain,
    w_out,
    ffn_gain,
    w_gate,
    w_up,
    w_down,
    cotangent,
):
    xl = lax.axis_index("xl")
    co = lax.axis_index("co")
    y = lax.axis_index("y")
    block = lax.axis_index("z") * 8 + y * 2 + lax.axis_index("xh")

    gains = jnp.concatenate([attn_gain, ffn_gain, query_gain, key_gain])
    gains = jnp.concatenate([gains, jnp.zeros((1024 - 576,), LOW)]).reshape(1, 8, 128)
    pair = jnp.concatenate([gains, x_pair(gains)], axis=0)
    pair = jnp.where(xl == 0, pair, pair[::-1])
    swapped = core_swap(pair)
    quad = jnp.where(co == 0, jnp.stack([pair, swapped], 1), jnp.stack([swapped, pair], 1))
    quad = quad.reshape(4, 1024).astype(F32)
    gain_one = quad[:, :256].reshape(1024)
    gain_two = quad[:, 256:512].reshape(1024)
    gain_query = quad[:, 512:544].reshape(128)
    gain_key = quad[:, 544:576].reshape(128)

    qkv_full, arrived = gather_weight(jnp.concatenate([w_query, w_key, w_value], axis=1))
    w_out, w_down, w_gate, w_up, _, _ = lax.optimization_barrier(
        (w_out, w_down, w_gate, w_up) + arrived
    )
    out_full, _ = gather_weight(w_out)
    gate_up_full, _ = gather_weight(jnp.concatenate([w_gate, w_up], axis=1))
    down_full, _ = gather_weight(w_down)

    start = block * ROWS + ROWS - 1 - positions[ROWS - 1]
    info = jnp.stack([start, y]).astype(jnp.int32)
    cosine, sine = rotary_tables(positions)
    inputs = tokens.astype(F32)
    scale_one = rms_scale(inputs)
    normal_one = inputs * scale_one
    normed_one = (normal_one * gain_one).astype(LOW)
    qkv = dot(normed_one, qkv_full)
    query_raw = qkv[:, :2048].reshape(ROWS, 16, HEAD)
    key_raw = qkv[:, 2048:3072].reshape(ROWS, 8, HEAD)
    value = qkv[:, 3072:].astype(LOW).reshape(ROWS, 8, HEAD)
    scale_q = rms_scale(query_raw)
    unit_q = query_raw * scale_q
    query = rotate_forward(unit_q * gain_query, cosine, sine).astype(LOW)
    scale_k = rms_scale(key_raw)
    unit_k = key_raw * scale_k
    key = rotate_forward(unit_k * gain_key, cosine, sine).astype(LOW)

    kv_send = jnp.transpose(jnp.concatenate([key, value], axis=-1), (1, 0, 2))
    kv = exchange_heads(kv_send)
    kv = exchange_y(jnp.broadcast_to(kv[None], (4,) + kv.shape))
    kv = jnp.transpose(kv.reshape(4, 4, 2, ROWS, 2 * HEAD), (1, 0, 2, 3, 4)).reshape(-1, 2 * HEAD)
    k_all, v_all = kv[:, :HEAD], kv[:, HEAD:]
    chunks = k_all.shape[0] // CHUNK
    kt_all = jnp.transpose(k_all.reshape(chunks, CHUNK, HEAD), (0, 2, 1))
    vt_all = jnp.transpose(v_all.reshape(chunks, CHUNK, HEAD), (0, 2, 1))
    q_send = jnp.transpose(query.reshape(ROWS, 8, 2, HEAD), (1, 2, 0, 3)).reshape(8, 2 * ROWS, HEAD)
    q_all = exchange_heads(q_send)
    mixed_t, logs = attention_forward(info, q_all, k_all, vt_all)

    o_send = jnp.transpose(mixed_t, (0, 2, 1)).astype(LOW)
    merged = exchange_heads(o_send).reshape(8, 2, ROWS, HEAD)
    merged = jnp.transpose(merged, (2, 0, 1, 3)).reshape(ROWS, 2048)

    middle = inputs + dot(merged, out_full)
    scale_two = rms_scale(middle)
    normal_two = middle * scale_two
    normed_two = (normal_two * gain_two).astype(LOW)
    gate_up = dot(normed_two, gate_up_full)
    gate_value, up_value = gate_up[:, :3072], gate_up[:, 3072:]
    gate_sigmoid = jax.nn.sigmoid(gate_value)
    swish = gate_value * gate_sigmoid
    hidden = (swish * up_value).astype(LOW)
    output = (middle + dot(hidden, down_full)).astype(LOW)
    grad_hidden = dot_t(cotangent, down_full)
    grad_gate = (
        grad_hidden * up_value * gate_sigmoid * (1.0 + gate_value * (1.0 - gate_sigmoid))
    ).astype(LOW)
    grad_up = (grad_hidden * swish).astype(LOW)
    feed_grads = jnp.concatenate([grad_gate, grad_up], axis=1)
    grad_normed_two = dot_t(feed_grads, gate_up_full)
    gain_two_term = jnp.sum(grad_normed_two * normal_two, axis=0)
    grad_middle = cotangent.astype(F32) + norm_back(
        grad_normed_two * gain_two, normal_two, scale_two
    )
    grad_branch = grad_middle.astype(LOW)
    grad_merged = dot_t(grad_branch, out_full).astype(LOW)

    left_two = both_cores_columns(normed_two, co)
    left_hidden = both_cores_columns(hidden, co).reshape(2 * ROWS, 2, 3, 256)
    left_merged = both_cores_columns(merged, co).reshape(2 * ROWS, 2, 2, 256)
    right_feed = both_cores(feed_grads)
    right_cot = both_cores(cotangent)
    right_branch = both_cores(grad_branch)
    pieces = [over_rows(left_two, right_feed).astype(LOW)]
    for g in range(3):
        pieces.append(over_rows(left_hidden[:, :, g].reshape(2 * ROWS, 512), right_cot).astype(LOW))
    for g in range(2):
        pieces.append(
            over_rows(left_merged[:, :, g].reshape(2 * ROWS, 512), right_branch).astype(LOW)
        )
    feed_first, feed_second = sum_everywhere(jnp.concatenate(pieces, axis=1))

    do_send = jnp.transpose(grad_merged.reshape(ROWS, 8, 2, HEAD), (1, 2, 0, 3))
    do_all = exchange_heads(do_send.reshape(8, 2 * ROWS, HEAD))
    dq_all, dkv_all = attention_backward(
        info, q_all, do_all, mixed_t, logs, k_all, kt_all, v_all
    )
    dkv = jnp.transpose(dkv_all.reshape(4, 4, 2, ROWS, 2 * HEAD), (1, 0, 2, 3, 4))
    dkv = exchange_y(dkv.reshape(4, 8, ROWS, 2 * HEAD))
    dkv = jnp.sum(dkv.astype(F32), axis=0).astype(LOW)
    dq_send = jnp.transpose(dq_all.reshape(8, 2, ROWS, HEAD), (0, 2, 1, 3))
    back = exchange_heads(
        jnp.concatenate([dq_send.reshape(8, ROWS, 2 * HEAD), dkv], axis=-1)
    )
    back = jnp.transpose(back, (1, 0, 2))
    grad_q = back[:, :, : 2 * HEAD].reshape(ROWS, 16, HEAD).astype(F32)
    grad_k = back[:, :, 2 * HEAD : 3 * HEAD].astype(F32)
    grad_value = back[:, :, 3 * HEAD :].reshape(ROWS, 1024)

    grad_scaled_q = rotate_back(grad_q, cosine, sine)
    query_gain_term = jnp.sum(grad_scaled_q * unit_q, axis=(0, 1))
    grad_query = norm_back(grad_scaled_q * gain_query, unit_q, scale_q).reshape(ROWS, 2048)
    grad_scaled_k = rotate_back(grad_k, cosine, sine)
    key_gain_term = jnp.sum(grad_scaled_k * unit_k, axis=(0, 1))
    grad_key = norm_back(grad_scaled_k * gain_key, unit_k, scale_k).reshape(ROWS, 1024)
    attention_grads = jnp.concatenate(
        [grad_query.astype(LOW), grad_key.astype(LOW), grad_value], axis=1
    )
    grad_normed_one = dot_t(attention_grads, qkv_full)
    gain_one_term = jnp.sum(grad_normed_one * normal_one, axis=0)
    grad_tokens = grad_middle + norm_back(grad_normed_one * gain_one, normal_one, scale_one)

    gain_terms = jnp.concatenate([gain_one_term, gain_two_term, query_gain_term, key_gain_term])
    gain_terms = gain_terms.reshape(18, 128)
    gain_terms = gain_terms + core_swap(gain_terms)
    gain_terms = jnp.pad(gain_terms, ((0, 238), (0, 128))).astype(LOW)
    gain_terms = jnp.concatenate([gain_terms, gain_terms], axis=0)
    left_one = both_cores_columns(normed_one, co)
    right_attention = both_cores(attention_grads)
    attention_part = jnp.concatenate(
        [over_rows(left_one, right_attention).astype(LOW), gain_terms], axis=1
    )
    qkv_first, qkv_second = sum_everywhere(attention_part)

    feed = jnp.concatenate([feed_first, feed_second], axis=1)
    grad_down = jnp.concatenate([feed[:, 6144 + 1024 * g : 7168 + 1024 * g] for g in range(3)], axis=0)
    grad_out = jnp.concatenate([feed[:, 9216 + 1024 * g : 10240 + 1024 * g] for g in range(2)], axis=0)
    wide = jnp.concatenate([qkv_first, qkv_second], axis=1)
    shard = xl * 2 + co
    gain_all = wide[:18, 4096:4224].reshape(2304)
    return (
        output,
        grad_tokens,
        lax.dynamic_slice_in_dim(gain_all, shard * 256, 256),
        wide[:, :2048],
        wide[:, 2048:3072],
        wide[:, 3072:4096],
        lax.dynamic_slice_in_dim(gain_all, 2048 + shard * 32, 32),
        lax.dynamic_slice_in_dim(gain_all, 2176 + shard * 32, 32),
        grad_out,
        lax.dynamic_slice_in_dim(gain_all, 1024 + shard * 256, 256),
        feed[:, :3072],
        feed[:, 3072:6144],
        grad_down,
    )


def x_pair(value):
    return lax.ppermute(value, "xl", [(0, 1), (1, 0)])


def solution(mesh):
    axes = ("xl", "co", "z", "y", "xh")
    fine = Mesh(mesh.devices.reshape(2, 2, 4, 4, 2), axes)
    rows = P(axes, None)
    shard = P(("xl", "co"), None)
    vector = P(("xl", "co"))
    in_specs = (
        rows,
        P(axes),
        vector,
        shard,
        shard,
        shard,
        vector,
        vector,
        shard,
        vector,
        shard,
        shard,
        shard,
        rows,
    )
    out_specs = (
        rows,
        rows,
        vector,
        shard,
        shard,
        shard,
        vector,
        vector,
        shard,
        vector,
        shard,
        shard,
        shard,
    )
    return jax.shard_map(local, mesh=fine, in_specs=in_specs, out_specs=out_specs, check_vma=False)
```

time: 2390 us -> 711 us (0.30)
  waiting for transfers between devices: 1140 us -> 186 us
  starting transfers between devices: 653 us -> 161 us
  blocking collectives: 126 us -> 0 us
  other arithmetic: 159 us -> 59 us
  Pallas kernels: 0 us -> 34.7 us
  loops' own time: 34.5 us -> 0 us
    ppermute x128 -> x87, starting transfers between devices: 653 us -> 115 us  [the longest x48 80.9 us: shift(): return lax.ppermute(value, axis, [(i, (i + step) % 4) for i in range(4)])]
    all_gather x9 -> x0, waiting for transfers between devices: 455 us -> none  [the longest x1 99 us: local(): lax.all_gather(key_flat, 'ctx', axis=0, tiled=True)]
    psum x1 -> x0, waiting for transfers between devices: 295 us -> none  [local(): lax.psum(input_part, 'ctx').astype(jnp.float32)]
    reduce_scatter x3 -> x0, waiting for transfers between devices: 214 us -> none  [the longest x1 214 us: local(): lax.psum_scatter(jnp.concatenate([first_part, second_part], axis=1).astyp...]
    psum x1 -> x0, blocking collectives: 97.5 us -> none  [local(): lax.psum(gain_parts[0].astype(jnp.bfloat16), 'ctx').astype(jnp.float32)]
    convert_element_type x146 -> x16, other arithmetic: 92.3 us -> 14 us  [the longest x6 6.24 us: reduce_over(): return total.astype(LOW)]
    while x75 -> x0, local copies, waits for them, and re-layouts: 77.4 us -> none
    dynamic_update_slice x0 -> x36, local copies, waits for them, and re-layouts: none -> 49.9 us  [the longest x24 49.7 us: gather_weight(): out = lax.dynamic_update_slice_in_dim(out, piece, at, 0)]
  transfers between devices with their start and end apart: 141 -> 94, of which waited for: 75 -> 38; matrix products, arithmetic and copies ran while one was open for 16% -> 42% of each run, Pallas kernels for 0% -> 5%
where the time goes in v1:
time: 711 us; the launch traced here: 699 us
  local copies, waits for them, and re-layouts  190 us (27%)
  waiting for transfers between devices  186 us (26%)
  starting transfers between devices  161 us (23%)
  matrix products  65.3 us (9%)
  other arithmetic  59 us (8%)
  Pallas kernels  34.7 us (5%)
    ppermute x48, waiting for transfers between devices, shift(): return lax.ppermute(value, axis, [(i, (i + step) % 4) for i in range(4)])  148 us
    ppermute x48, starting transfers between devices, shift(): return lax.ppermute(value, axis, [(i, (i + step) % 4) for i in range(4)])  80.9 us
    dynamic_update_slice x24, local copies, waits for them, and re-layouts, gather_weight(): out = lax.dynamic_update_slice_in_dim(out, piece, at, 0)  49.7 us
    unnamed x187, local copies, waits for them, and re-layouts  33 us
    all_to_all x5, starting transfers between devices, exchange_heads(): lax.all_to_all(value, ('z', 'xh'), split_axis=0, concat_axis=0, tiled=True)  31.3 us
    dot_general x4, matrix products, dot_t(): lax.dot_general(left, right, (((1,), (1,)), ((), ())), preferred_element_...  23.3 us
    ppermute x14, starting transfers between devices, x_shift(): return lax.ppermute(value, ('xl', 'xh'), pairs)  23.2 us
    dot_general x7, matrix products, over_rows(): lax.dot_general(left, right, (((0,), (0,)), ((), ())), preferred_element_...  22.3 us
  transfers between devices with their start and end apart: 94, of which 38 were waited for; matrix products, arithmetic and copies ran while one was open for 42% of the time, Pallas kernels for 5%

profile of v1, /device:TPU:0, one launch (start us, length us, event | category | flops | bytes accessed | tf_op | source)
XLA Modules:
  0.0 699.0 jit_solution(9357965358998594441)
XLA Ops:
  58.2 6.1 broadcast_in_dim.187
  78.8 4.6 constant_dynamic-update-slice_fusion.27
  87.4 4.6 fusion.114
  115.8 5.3 all-to-all-start.1
  153.5 12.0 %all-to-all-done.2 = bf16[4,8,128,256]{3,2,1,0:T(8,128)(2,1)S(1)} async-done(((bf16[4,8,128,256]{3,2,1,0:T(8,128)(2,1)}), bf16[4,8,128,256]{3,2,1,0:T(8,128)(2,1)S(1)}, u32[]{:S(2)}, u32[]{:S(2)}) %all-to-all-start.2) | async-done | bytes 2097184 | tf_op jit(solution)/shard_map/all_to_all | solution.py:310
  165.5 7.2 %all-to-all-start = ((bf16[8,256,128]{2,1,0:T(8,128)(2,1)}), bf16[8,256,128]{2,1,0:T(8,128)(2,1)S(1)}, u32[]{:S(2)}, u32[]{:S(2)}) async-start(bf16[8,256,128]{2,1,0:T(8,128)(2,1)} %bitcast.10), calls=%async_computation | async-start | bytes 1048576 | tf_op jit(solution)/shard_map/all_to_all | solution.py:306
  174.3 9.1 %all-to-all-done.q_ref = bf16[8,256,128]{2,1,0:T(8,128)(2,1)S(1)} async-done(((bf16[8,256,128]{2,1,0:T(8,128)(2,1)}), bf16[8,256,128]{2,1,0:T(8,128)(2,1)S(1)}, u32[]{:S(2)}, u32[]{:S(2)}) %all-to-all-start) | async-done | bytes 524320 | tf_op jit(solution)/shard_map/all_to_all | solution.py:306
  186.5 15.2 %attention_forward.1 = (f32[8,128,256]{2,1,0:T(8,128)S(1)}, f32[8,1,256]{2,1,0:T(1,128)S(1)}) custom-call(s32[2]{0:T(128)S(1)} %pad_add_fusion.info, bf16[8,256,128]{2,1,0:T(8,128)(2,1)S(1)} %copy-done.3, bf16[4096,128]{1,0:T(8,128)(2,1)S(1)} %get-tuple-element.77.k_ref, bf16[8,128,512]{2,1,0:T(8,128)(2,1)S(1)} %bitcast.387), custom_call_target="tpu_custom_call" | custom-call | flops 3000000000 | bytes 5242880 | tf_op jit(solution)/shard_map/attention_forward/pallas_call | solution.py:215
  222.8 7.1 %fusion.115 = f32[128,6144]{1,0:T(8,128)S(1)} fusion(bf16[128,1024]{1,0:T(8,128)(2,1)S(1)} %multiply_convert_fusion.4, bf16[1024,6144]{1,0:T(8,128)(2,1)} %constant_dynamic-update-slice_fusion.13), kind=kOutput, calls=%fused_computation.337 | convolution fusion | flops 1610612736 | bytes 15990784 | tf_op jit(solution)/shard_map/dot_general | solution.py:302
  234.4 10.1 %multiply_reduce_fusion.3 = (f32[1024]{0:T(1024)}, f32[128]{0:T(128)S(1)}, f32[128,1024]{1,0:T(8,128)S(1)}) fusion(f32[128,1024]{1,0:T(8,128)S(1)} %get-tuple-element.142, f32[128]{0:T(128)S(1)} %add_rsqrt_fusion.2, f32[1024]{0:T(1024)S(1)} %bitcast.451, bf16[1024,6144]{1,0:T(8,128)(2,1)} %constant_dynamic-update-slice_fusion.13, ...), kind=kOutput, calls=%fused_computation.151 | convolution fusion | flops 1614543744 | bytes 15213568 | tf_op jit(solution)/shard_map/dot_general | solution.py:124
  254.9 7.1 %all-to-all-start.4 = ((bf16[8,256,128]{2,1,0:T(8,128)(2,1)}), bf16[8,256,128]{2,1,0:T(8,128)(2,1)}, u32[]{:S(2)}, u32[]{:S(2)}) async-start(bf16[8,256,128]{2,1,0:T(8,128)(2,1)} %bitcast.426), calls=%async_computation.4 | async-start | bytes 1048576 | tf_op jit(solution)/shard_map/all_to_all | solution.py:306
  275.1 4.8 fusion.25
  297.4 19.5 %attention_backward.1 = (bf16[8,256,128]{2,1,0:T(8,128)(2,1)S(1)}, bf16[4096,256]{1,0:T(8,128)(2,1)S(1)}) custom-call(s32[2]{0:T(128)S(1)} %pad_add_fusion.info, bf16[8,256,128]{2,1,0:T(8,128)(2,1)S(1)} %copy-done.4, bf16[8,256,128]{2,1,0:T(8,128)(2,1)} %all-to-all-done.4.do_ref, f32[8,128,256]{2,1,0:T(8,128)S(1)} %get-tuple-element.21.ot_ref, ...), custom_call_target="tpu_custom_call" | custom-call | flops 8000000000 | bytes 10485760 | tf_op jit(solution)/shard_map/attention_backward/pallas_call | solution.py:239
  318.4 10.3 %all-to-all-start.5 = ((bf16[4,8,128,256]{3,2,1,0:T(8,128)(2,1)}), bf16[4,8,128,256]{3,2,1,0:T(8,128)(2,1)S(1)}, u32[]{:S(2)}, u32[]{:S(2)}) async-start(bf16[4,8,128,256]{3,2,1,0:T(8,128)(2,1)} %bitcast.413), calls=%async_computation.5 | async-start | bytes 4194304 | tf_op jit(solution)/shard_map/all_to_all | solution.py:310
  329.2 6.5 fusion
  345.1 9.5 %fusion.99 = (bf16[2,4,4,16,5632]{4,3,2,1,0:T(8,128)(2,1)}, bf16[2,4,4,16,5632]{4,3,2,1,0:T(8,128)(2,1)}) fusion(bf16[2,4,4,16,11264]{4,3,2,1,0:T(8,128)(2,1)} %bitcast.104), kind=kLoop, calls=%fused_computation.321 | loop fusion | bytes 23068672 | tf_op jit(solution)/shard_map/slice | solution.py:72
  357.0 7.3 %all-to-all-start.6 = ((bf16[8,128,512]{2,1,0:T(8,128)(2,1)}), bf16[8,128,512]{2,1,0:T(8,128)(2,1)S(1)}, u32[]{:S(2)}, u32[]{:S(2)}) async-start(bf16[8,128,512]{2,1,0:T(8,128)(2,1)} %pad_maximum_fusion.5), calls=%async_computation.6 | async-start | bytes 2097152 | tf_op jit(solution)/shard_map/all_to_all | solution.py:306
  401.9 6.5 fusion.57
  414.2 25.2 %collective-permute-done.66 = bf16[2,4,16,5632]{3,2,1,0:T(8,128)(2,1)} collective-permute-done((bf16[2,4,16,5632]{3,2,1,0:T(8,128)(2,1)}, bf16[2,4,16,5632]{3,2,1,0:T(8,128)(2,1)}, u32[]{:S(2)}, u32[]{:S(2)}) %collective-permute-start.66) | collective-permute-done | bytes 1441824 | tf_op jit(solution)/shard_map/ppermute | solution.py:32
  448.8 25.1 %collective-permute-done.59 = bf16[2,4,16,5632]{3,2,0,1:T(8,128)(2,1)S(1)} collective-permute-done((bf16[2,4,16,5632]{3,2,0,1:T(8,128)(2,1)S(1)}, bf16[2,4,16,5632]{3,2,0,1:T(8,128)(2,1)S(1)}, u32[]{:S(2)}, u32[]{:S(2)}) %collective-permute-start.59) | collective-permute-done | bytes 1441824 | tf_op jit(solution)/shard_map/ppermute | solution.py:32
  477.8 6.2 collective-permute-done.70
  493.2 8.5 %collective-permute-done.63 = bf16[2,16,5632]{2,1,0:T(8,128)(2,1)S(1)} collective-permute-done((bf16[2,16,5632]{2,1,0:T(8,128)(2,1)S(1)}, bf16[2,16,5632]{2,1,0:T(8,128)(2,1)S(1)}, u32[]{:S(2)}, u32[]{:S(2)}) %collective-permute-start.63) | collective-permute-done | bytes 360480 | tf_op jit(solution)/shard_map/ppermute | solution.py:32
  525.2 7.2 %collective-permute-done.75 = bf16[16,5632]{1,0:T(8,128)(2,1)S(1)} collective-permute-done((bf16[16,5632]{1,0:T(8,128)(2,1)S(1)}, bf16[16,5632]{1,0:T(8,128)(2,1)S(1)}, u32[]{:S(2)}, u32[]{:S(2)}) %collective-permute-start.75) | collective-permute-done | bytes 180256 | tf_op jit(solution)/shard_map/ppermute | solution.py:32
  546.5 6.5 convolution_convert_fusion.1
  553.0 8.2 %maximum_maximum_fusion = bf16[512,4352]{1,0:T(8,128)(2,1)S(1)} fusion(bf16[256,256]{1,0:T(8,128)(2,1)S(1)} %pad.5, bf16[512,4096]{1,0:T(8,128)(2,1)S(1)} %convolution_convert_fusion.1), kind=kLoop, calls=%fused_computation.3 | loop fusion | flops 13369344 | bytes 8781824 | tf_op jit(solution)/shard_map/concatenate | solution.py:481
  565.4 10.8 %collective-permute-done.27 = bf16[2,4,16,2176]{3,2,0,1:T(8,128)(2,1)S(1)} collective-permute-done((bf16[2,4,16,2176]{3,2,0,1:T(8,128)(2,1)S(1)}, bf16[2,4,16,2176]{3,2,0,1:T(8,128)(2,1)S(1)}, u32[]{:S(2)}, u32[]{:S(2)}) %collective-permute-start.27) | collective-permute-done | bytes 557088 | tf_op jit(solution)/shard_map/ppermute | solution.py:32
  576.2 7.3 %collective-permute-done.26 = bf16[2,4,16,2176]{3,2,0,1:T(8,128)(2,1)S(1)} collective-permute-done((bf16[2,4,16,2176]{3,2,0,1:T(8,128)(2,1)S(1)}, bf16[2,4,16,2176]{3,2,0,1:T(8,128)(2,1)S(1)}, u32[]{:S(2)}, u32[]{:S(2)}) %collective-permute-start.26) | collective-permute-done | bytes 557088 | tf_op jit(solution)/shard_map/ppermute | solution.py:32
  590.0 9.1 %collective-permute-done.32 = bf16[2,4,16,2176]{3,2,1,0:T(8,128)(2,1)S(1)} collective-permute-done((bf16[2,4,16,2176]{3,2,1,0:T(8,128)(2,1)S(1)}, bf16[2,4,16,2176]{3,2,1,0:T(8,128)(2,1)S(1)}, u32[]{:S(2)}, u32[]{:S(2)}) %collective-permute-start.32) | collective-permute-done | bytes 557088 | tf_op jit(solution)/shard_map/ppermute | solution.py:32
  599.3 16.0 %collective-permute-done.31 = bf16[2,4,16,2176]{3,2,1,0:T(8,128)(2,1)S(1)} collective-permute-done((bf16[2,4,16,2176]{3,2,1,0:T(8,128)(2,1)S(1)}, bf16[2,4,16,2176]{3,2,1,0:T(8,128)(2,1)S(1)}, u32[]{:S(2)}, u32[]{:S(2)}) %collective-permute-start.31) | collective-permute-done | bytes 557088 | tf_op jit(solution)/shard_map/ppermute | solution.py:32
  623.9 11.2 %collective-permute-start.34 = (bf16[2,16,2176]{2,1,0:T(8,128)(2,1)S(1)}, bf16[2,16,2176]{2,1,0:T(8,128)(2,1)S(1)}, u32[]{:S(2)}, u32[]{:S(2)}) collective-permute-start(bf16[2,16,2176]{2,1,0:T(8,128)(2,1)S(1)} %get-tuple-element.113), channel_id=1, source_target_pairs={{0,2},{2,4},{4,6},{6,0},{1,3},{3,5},{5,7},{7,1},{8,10},{10,12},{12... | collective-permute-start | bytes 417800 | tf_op jit(solution)/shard_map/ppermute | solution.py:32
  635.2 6.4 collective-permute-done.85
  648.2 4.7 collective-permute-done.28
  (572 shorter events, 390.6 us)
Async XLA Ops:
  7.5 71.0 %collective-permute-start.4 = (bf16[256,4096]{1,0:T(8,128)(2,1)S(1)}, bf16[256,4096]{1,0:T(8,128)(2,1)}, u32[]{:S(2)}, u32[]{:S(2)}) collective-permute-start(bf16[256,4096]{1,0:T(8,128)(2,1)S(1)} %constant_dynamic-update-slice_fusion), channel_id=1, source_target_pairs={{0,32},{32,0},{1,33},{33,1},{2,34},{34,2},{3,35},{35,3},{4,36},{36... | collective-permute-start | bytes 6291464 | tf_op jit(solution)/shard_map/ppermute | solution.py:36
  9.1 30.0 %collective-permute-start.2 = (bf16[128,4096]{1,0:T(8,128)(2,1)}, bf16[128,4096]{1,0:T(8,128)(2,1)}, u32[]{:S(2)}, u32[]{:S(2)}) collective-permute-start(bf16[128,4096]{1,0:T(8,128)(2,1)} %get-tuple-element.83), channel_id=1, source_target_pairs={{0,64},{64,1},{1,65},{65,0},{2,66},{66,3},{3,67},{67,2},{4,68},{68... | collective-permute-start | bytes 3145736 | tf_op jit(solution)/shard_map/ppermute | solution.py:26
  41.5 31.4 %collective-permute-start.7 = (bf16[256,1024]{1,0:T(8,128)(2,1)}, bf16[256,1024]{1,0:T(8,128)(2,1)}, u32[]{:S(2)}, u32[]{:S(2)}) collective-permute-start(bf16[256,1024]{1,0:T(8,128)(2,1)} %get-tuple-element.99), channel_id=1, source_target_pairs={{0,64},{64,1},{1,65},{65,0},{2,66},{66,3},{3,67},{67,2},{4,68},{68... | collective-permute-start | bytes 1572872 | tf_op jit(solution)/shard_map/ppermute | solution.py:26
  41.5 34.5 %collective-permute-start.8 = (bf16[256,1024]{1,0:T(8,128)(2,1)}, bf16[256,1024]{1,0:T(8,128)(2,1)}, u32[]{:S(2)}, u32[]{:S(2)}) collective-permute-start(bf16[256,1024]{1,0:T(8,128)(2,1)} %get-tuple-element.98), channel_id=1, source_target_pairs={{0,65},{64,0},{1,64},{65,1},{2,67},{66,2},{3,66},{67,3},{4,69},{68... | collective-permute-start | bytes 1572872 | tf_op jit(solution)/shard_map/ppermute | solution.py:26
  76.0 30.6 %collective-permute-start.9 = (bf16[512,1024]{1,0:T(8,128)(2,1)}, bf16[512,1024]{1,0:T(8,128)(2,1)}, u32[]{:S(2)}, u32[]{:S(2)}) collective-permute-start(bf16[512,1024]{1,0:T(8,128)(2,1)} %param.22), channel_id=1, source_target_pairs={{0,32},{32,0},{1,33},{33,1},{2,34},{34,2},{3,35},{35,3},{4,36},{36... | collective-permute-start | bytes 3145736 | tf_op jit(solution)/shard_map/ppermute | solution.py:36
  77.7 62.4 %collective-permute-start.19 = (bf16[768,1024]{1,0:T(8,128)(2,1)}, bf16[768,1024]{1,0:T(8,128)(2,1)}, u32[]{:S(2)}, u32[]{:S(2)}) collective-permute-start(bf16[768,1024]{1,0:T(8,128)(2,1)} %param.26), channel_id=1, source_target_pairs={{0,32},{32,0},{1,33},{33,1},{2,34},{34,2},{3,35},{35,3},{4,36},{36... | collective-permute-start | bytes 4718600 | tf_op jit(solution)/shard_map/ppermute | solution.py:36
  78.5 64.3 %collective-permute-start.12 = (bf16[128,6144]{1,0:T(8,128)(2,1)}, bf16[128,6144]{1,0:T(8,128)(2,1)}, u32[]{:S(2)}, u32[]{:S(2)}) collective-permute-start(bf16[128,6144]{1,0:T(8,128)(2,1)} %get-tuple-element.66), channel_id=1, source_target_pairs={{0,64},{64,1},{1,65},{65,0},{2,66},{66,3},{3,67},{67,2},{4,68},{68... | collective-permute-start | bytes 4718600 | tf_op jit(solution)/shard_map/ppermute | solution.py:26
  83.4 60.0 %collective-permute-start.13 = (bf16[128,6144]{1,0:T(8,128)(2,1)}, bf16[128,6144]{1,0:T(8,128)(2,1)}, u32[]{:S(2)}, u32[]{:S(2)}) collective-permute-start(bf16[128,6144]{1,0:T(8,128)(2,1)} %get-tuple-element.65), channel_id=1, source_target_pairs={{0,65},{64,0},{1,64},{65,1},{2,67},{66,2},{3,66},{67,3},{4,69},{68... | collective-permute-start | bytes 4718600 | tf_op jit(solution)/shard_map/ppermute | solution.py:26
  86.3 37.5 %collective-permute-start.10 = (bf16[256,1024]{1,0:T(8,128)(2,1)}, bf16[256,1024]{1,0:T(8,128)(2,1)}, u32[]{:S(2)}, u32[]{:S(2)}) collective-permute-start(bf16[256,1024]{1,0:T(8,128)(2,1)} %collective-permute-done.7), channel_id=1, source_target_pairs={{0,32},{32,0},{1,33},{33,1},{2,34},{34,2},{3,35},{35,3},{4,36},{36... | collective-permute-start | bytes 1572872 | tf_op jit(solution)/shard_map/ppermute | solution.py:36
  140.1 406.4 %collective-permute-start.22 = (bf16[128,512]{0,1:T(8,128)(2,1)}, bf16[128,512]{0,1:T(8,128)(2,1)}, u32[]{:S(2)}, u32[]{:S(2)}) collective-permute-start(bf16[128,512]{0,1:T(8,128)(2,1)} %bitcast.38), channel_id=1, source_target_pairs={{0,32},{32,0},{1,33},{33,1},{2,34},{34,2},{3,35},{35,3},{4,36},{36... | collective-permute-start | bytes 393224 | tf_op jit(solution)/shard_map/ppermute | solution.py:36
  142.8 65.4 %collective-permute-start.14 = (bf16[256,6144]{1,0:T(8,128)(2,1)}, bf16[256,6144]{1,0:T(8,128)(2,1)}, u32[]{:S(2)}, u32[]{:S(2)}) collective-permute-start(bf16[256,6144]{1,0:T(8,128)(2,1)} %constant_dynamic-update-slice_fusion.3), channel_id=1, source_target_pairs={{0,32},{32,0},{1,33},{33,1},{2,34},{34,2},{3,35},{35,3},{4,36},{36... | collective-permute-start | bytes 9437192 | tf_op jit(solution)/shard_map/ppermute | solution.py:36
  143.4 68.8 %collective-permute-start.15 = (bf16[128,6144]{1,0:T(8,128)(2,1)}, bf16[128,6144]{1,0:T(8,128)(2,1)}, u32[]{:S(2)}, u32[]{:S(2)}) collective-permute-start(bf16[128,6144]{1,0:T(8,128)(2,1)} %collective-permute-done.12), channel_id=1, source_target_pairs={{0,32},{32,0},{1,33},{33,1},{2,34},{34,2},{3,35},{35,3},{4,36},{36... | collective-permute-start | bytes 4718600 | tf_op jit(solution)/shard_map/ppermute | solution.py:36
  143.5 71.4 %collective-permute-start.16 = (bf16[128,6144]{1,0:T(8,128)(2,1)}, bf16[128,6144]{1,0:T(8,128)(2,1)}, u32[]{:S(2)}, u32[]{:S(2)}) collective-permute-start(bf16[128,6144]{1,0:T(8,128)(2,1)} %collective-permute-done.13), channel_id=1, source_target_pairs={{0,32},{32,0},{1,33},{33,1},{2,34},{34,2},{3,35},{35,3},{4,36},{36... | collective-permute-start | bytes 4718600 | tf_op jit(solution)/shard_map/ppermute | solution.py:36
  254.9 40.2 %all-to-all-start.4 = ((bf16[8,256,128]{2,1,0:T(8,128)(2,1)}), bf16[8,256,128]{2,1,0:T(8,128)(2,1)}, u32[]{:S(2)}, u32[]{:S(2)}) async-start(bf16[8,256,128]{2,1,0:T(8,128)(2,1)} %bitcast.426), calls=%async_computation.4 | async-start | bytes 1048576 | tf_op jit(solution)/shard_map/all_to_all | solution.py:306
  262.0 67.2 %collective-permute-start.54 = (bf16[128,6144]{1,0:T(8,128)(2,1)}, bf16[128,6144]{1,0:T(8,128)(2,1)}, u32[]{:S(2)}, u32[]{:S(2)}) collective-permute-start(bf16[128,6144]{1,0:T(8,128)(2,1)} %pad_maximum_fusion.3), channel_id=1, source_target_pairs={{0,32},{32,0},{1,33},{33,1},{2,34},{34,2},{3,35},{35,3},{4,36},{36... | collective-permute-start | bytes 4718600 | tf_op jit(solution)/shard_map/ppermute | solution.py:36
  281.7 58.5 %collective-permute-start.58 = (bf16[128,1024]{1,0:T(8,128)(2,1)}, bf16[128,1024]{1,0:T(8,128)(2,1)}, u32[]{:S(2)}, u32[]{:S(2)}) collective-permute-start(bf16[128,1024]{1,0:T(8,128)(2,1)} %copy-done.41), channel_id=1, source_target_pairs={{0,32},{32,0},{1,33},{33,1},{2,34},{34,2},{3,35},{35,3},{4,36},{36... | collective-permute-start | bytes 786440 | tf_op jit(solution)/shard_map/ppermute | solution.py:36
  290.9 38.2 %collective-permute-start.53 = (bf16[128,512]{0,1:T(8,128)(2,1)}, bf16[128,512]{0,1:T(8,128)(2,1)}, u32[]{:S(2)}, u32[]{:S(2)}) collective-permute-start(bf16[128,512]{0,1:T(8,128)(2,1)} %bitcast.449), channel_id=1, source_target_pairs={{0,32},{32,0},{1,33},{33,1},{2,34},{34,2},{3,35},{35,3},{4,36},{36... | collective-permute-start | bytes 393224 | tf_op jit(solution)/shard_map/ppermute | solution.py:36
  318.4 37.2 %all-to-all-start.5 = ((bf16[4,8,128,256]{3,2,1,0:T(8,128)(2,1)}), bf16[4,8,128,256]{3,2,1,0:T(8,128)(2,1)S(1)}, u32[]{:S(2)}, u32[]{:S(2)}) async-start(bf16[4,8,128,256]{3,2,1,0:T(8,128)(2,1)} %bitcast.413), calls=%async_computation.5 | async-start | bytes 4194304 | tf_op jit(solution)/shard_map/all_to_all | solution.py:310
  368.9 42.7 %collective-permute-start.67 = (bf16[2,4,16,5632]{3,2,1,0:T(8,128)(2,1)}, bf16[2,4,16,5632]{3,2,1,0:T(8,128)(2,1)}, u32[]{:S(2)}, u32[]{:S(2)}) collective-permute-start(bf16[2,4,16,5632]{3,2,1,0:T(8,128)(2,1)} %get-tuple-element.58), channel_id=1, source_target_pairs={{0,16},{8,24},{16,0},{24,8},{1,17},{9,25},{17,1},{25,9},{2,18},{10... | collective-permute-start | bytes 4325384 | tf_op jit(solution)/shard_map/ppermute | solution.py:32
  372.4 67.0 %collective-permute-start.66 = (bf16[2,4,16,5632]{3,2,1,0:T(8,128)(2,1)}, bf16[2,4,16,5632]{3,2,1,0:T(8,128)(2,1)}, u32[]{:S(2)}, u32[]{:S(2)}) collective-permute-start(bf16[2,4,16,5632]{3,2,1,0:T(8,128)(2,1)} %get-tuple-element.59), channel_id=1, source_target_pairs={{0,24},{8,0},{16,8},{24,16},{1,25},{9,1},{17,9},{25,17},{2,26},{10... | collective-permute-start | bytes 4325384 | tf_op jit(solution)/shard_map/ppermute | solution.py:32
  373.6 67.4 %collective-permute-start.65 = (bf16[2,4,16,5632]{3,2,1,0:T(8,128)(2,1)}, bf16[2,4,16,5632]{3,2,1,0:T(8,128)(2,1)}, u32[]{:S(2)}, u32[]{:S(2)}) collective-permute-start(bf16[2,4,16,5632]{3,2,1,0:T(8,128)(2,1)} %get-tuple-element.57), channel_id=1, source_target_pairs={{0,8},{8,16},{16,24},{24,0},{1,9},{9,17},{17,25},{25,1},{2,10},{10... | collective-permute-start | bytes 4325384 | tf_op jit(solution)/shard_map/ppermute | solution.py:32
  377.2 67.3 %collective-permute-start.61 = (bf16[2,4,16,5632]{3,2,0,1:T(8,128)(2,1)}, bf16[2,4,16,5632]{3,2,0,1:T(8,128)(2,1)}, u32[]{:S(2)}, u32[]{:S(2)}) collective-permute-start(bf16[2,4,16,5632]{3,2,0,1:T(8,128)(2,1)} %bitcast.376), channel_id=1, source_target_pairs={{0,4},{2,6},{4,0},{6,2},{1,5},{3,7},{5,1},{7,3},{8,12},{10,14},{12... | collective-permute-start | bytes 4325384 | tf_op jit(solution)/shard_map/ppermute | solution.py:32
  411.7 35.9 %collective-permute-start.60 = (bf16[2,4,16,5632]{3,2,0,1:T(8,128)(2,1)S(1)}, bf16[2,4,16,5632]{3,2,0,1:T(8,128)(2,1)S(1)}, u32[]{:S(2)}, u32[]{:S(2)}) collective-permute-start(bf16[2,4,16,5632]{3,2,0,1:T(8,128)(2,1)S(1)} %bitcast.433), channel_id=1, source_target_pairs={{0,6},{2,0},{4,2},{6,4},{1,7},{3,1},{5,3},{7,5},{8,14},{10,8},{12,... | collective-permute-start | bytes 4325384 | tf_op jit(solution)/shard_map/ppermute | solution.py:32
  439.4 34.4 %collective-permute-start.59 = (bf16[2,4,16,5632]{3,2,0,1:T(8,128)(2,1)S(1)}, bf16[2,4,16,5632]{3,2,0,1:T(8,128)(2,1)S(1)}, u32[]{:S(2)}, u32[]{:S(2)}) collective-permute-start(bf16[2,4,16,5632]{3,2,0,1:T(8,128)(2,1)S(1)} %bitcast.432), channel_id=1, source_target_pairs={{0,2},{2,4},{4,6},{6,0},{1,3},{3,5},{5,7},{7,1},{8,10},{10,12},{12... | collective-permute-start | bytes 4325384 | tf_op jit(solution)/shard_map/ppermute | solution.py:32
  441.1 76.1 %collective-permute-start.24 = (f32[18,128]{1,0:T(8,128)S(1)}, f32[18,128]{1,0:T(8,128)S(1)}, u32[]{:S(2)}, u32[]{:S(2)}) collective-permute-start(f32[18,128]{1,0:T(8,128)S(1)} %maximum_bitcast_fusion.1), channel_id=1, source_target_pairs={{0,32},{32,0},{1,33},{33,1},{2,34},{34,2},{3,35},{35,3},{4,36},{36... | collective-permute-start | bytes 27656 | tf_op jit(solution)/shard_map/ppermute | solution.py:36
  444.6 39.4 %collective-permute-start.70 = (bf16[2,16,5632]{2,1,0:T(8,128)(2,1)S(1)}, bf16[2,16,5632]{2,1,0:T(8,128)(2,1)S(1)}, u32[]{:S(2)}, u32[]{:S(2)}) collective-permute-start(bf16[2,16,5632]{2,1,0:T(8,128)(2,1)S(1)} %get-tuple-element.90), channel_id=1, source_target_pairs={{0,4},{2,6},{4,0},{6,2},{1,5},{3,7},{5,1},{7,3},{8,12},{10,14},{12... | collective-permute-start | bytes 1081352 | tf_op jit(solution)/shard_map/ppermute | solution.py:32
  447.6 39.1 %collective-permute-start.69 = (bf16[2,16,5632]{2,1,0:T(8,128)(2,1)S(1)}, bf16[2,16,5632]{2,1,0:T(8,128)(2,1)S(1)}, u32[]{:S(2)}, u32[]{:S(2)}) collective-permute-start(bf16[2,16,5632]{2,1,0:T(8,128)(2,1)S(1)} %get-tuple-element.91), channel_id=1, source_target_pairs={{0,6},{2,0},{4,2},{6,4},{1,7},{3,1},{5,3},{7,5},{8,14},{10,8},{12,... | collective-permute-start | bytes 1081352 | tf_op jit(solution)/shard_map/ppermute | solution.py:32
  511.7 34.8 %collective-permute-start.23 = (bf16[128,4096]{1,0:T(8,128)(2,1)S(1)}, bf16[128,4096]{1,0:T(8,128)(2,1)S(1)}, u32[]{:S(2)}, u32[]{:S(2)}) collective-permute-start(bf16[128,4096]{1,0:T(8,128)(2,1)S(1)} %pad_maximum_fusion.7), channel_id=1, source_target_pairs={{0,32},{32,0},{1,33},{33,1},{2,34},{34,2},{3,35},{35,3},{4,36},{36... | collective-permute-start | bytes 3145736 | tf_op jit(solution)/shard_map/ppermute | solution.py:36
  541.0 78.7 %collective-permute-start.78 = (bf16[4,16,5632]{2,1,0:T(8,128)(2,1)S(1)}, bf16[4,16,5632]{2,1,0:T(8,128)(2,1)S(1)}, u32[]{:S(2)}, u32[]{:S(2)}) collective-permute-start(bf16[4,16,5632]{2,1,0:T(8,128)(2,1)S(1)} %bitcast_dynamic-update-slice_fusion.4), channel_id=1, source_target_pairs={{0,8},{8,16},{16,24},{24,0},{1,9},{9,17},{17,25},{25,1},{2,10},{10... | collective-permute-start | bytes 2162696 | tf_op jit(solution)/shard_map/ppermute | solution.py:32
  541.4 78.6 %collective-permute-start.79 = (bf16[4,16,5632]{2,1,0:T(8,128)(2,1)S(1)}, bf16[4,16,5632]{2,1,0:T(8,128)(2,1)S(1)}, u32[]{:S(2)}, u32[]{:S(2)}) collective-permute-start(bf16[4,16,5632]{2,1,0:T(8,128)(2,1)S(1)} %bitcast_dynamic-update-slice_fusion.4), channel_id=1, source_target_pairs={{0,24},{8,0},{16,8},{24,16},{1,25},{9,1},{17,9},{25,17},{2,26},{10... | collective-permute-start | bytes 2162696 | tf_op jit(solution)/shard_map/ppermute | solution.py:32
  583.8 31.6 %collective-permute-start.31 = (bf16[2,4,16,2176]{3,2,1,0:T(8,128)(2,1)S(1)}, bf16[2,4,16,2176]{3,2,1,0:T(8,128)(2,1)S(1)}, u32[]{:S(2)}, u32[]{:S(2)}) collective-permute-start(bf16[2,4,16,2176]{3,2,1,0:T(8,128)(2,1)S(1)} %get-tuple-element.73), channel_id=1, source_target_pairs={{0,8},{8,16},{16,24},{24,0},{1,9},{9,17},{17,25},{25,1},{2,10},{10... | collective-permute-start | bytes 1671176 | tf_op jit(solution)/shard_map/ppermute | solution.py:32
  590.0 33.7 %collective-permute-start.80 = (bf16[4,16,5632]{2,1,0:T(8,128)(2,1)S(1)}, bf16[4,16,5632]{2,1,0:T(8,128)(2,1)S(1)}, u32[]{:S(2)}, u32[]{:S(2)}) collective-permute-start(bf16[4,16,5632]{2,1,0:T(8,128)(2,1)S(1)} %bitcast_dynamic-update-slice_fusion.4), channel_id=1, source_target_pairs={{0,16},{8,24},{16,0},{24,8},{1,17},{9,25},{17,1},{25,9},{2,18},{10... | collective-permute-start | bytes 2162696 | tf_op jit(solution)/shard_map/ppermute | solution.py:32
  (144 other events, 1531.1 us)

commit v2 on v1

v2 whole, which is shorter than its diff:
```python
import jax
import jax.numpy as jnp
from jax import lax
from jax.experimental import pallas as pl
from jax.experimental.pallas import tpu as pltpu
from jax.sharding import Mesh
from jax.sharding import PartitionSpec as P

EPSILON = 1e-06
THETA = 1000000.0
HEAD = 128
ROWS = 128
CHUNK = 512
SCORE_SCALE = HEAD ** (-0.5)
LOG2_E = 1.4426950408889634
EXP_SCALE = SCORE_SCALE * LOG2_E
LOW = jnp.bfloat16
FEED_CUTS = ((0, 256), (1408, 1664), (256, 1408), (1664, 2816))
F32 = jnp.float32


def x_shift(value, step):
    pairs = []
    for x in range(4):
        to = (x + step) % 4
        pairs.append(((x % 2) * 2 + x // 2, (to % 2) * 2 + to // 2))
    return lax.ppermute(value, ("xl", "xh"), pairs)


def shift(value, axis, step):
    if axis == "x":
        return x_shift(value, step)
    return lax.ppermute(value, axis, [(i, (i + step) % 4) for i in range(4)])


def core_swap(value):
    return lax.ppermute(value, "co", [(0, 1), (1, 0)])


def place_on(axis):
    if axis == "x":
        return lax.axis_index("xh") * 2 + lax.axis_index("xl")
    return lax.axis_index(axis)


def pick(value, index, dim):
    return lax.dynamic_index_in_dim(value, index, dim, keepdims=False)


def send_parts(value, axis, dim):
    me = place_on(axis)
    got = [shift(pick(value, (me + step) % 4, dim), axis, step) for step in (1, 3, 2)]
    return [pick(value, me, dim)] + got


def add_parts(parts):
    total = parts[0].astype(F32)
    for part in parts[1:]:
        total = total + part.astype(F32)
    return total.astype(LOW)


def reduce_over(value, axis, dim):
    return add_parts(send_parts(value, axis, dim))


def gather_over(value, axis, dim, dtype=LOW):
    me = place_on(axis)
    shape = value.shape[:dim] + (4,) + value.shape[dim:]
    out = jnp.zeros(shape, dtype)
    out = lax.dynamic_update_index_in_dim(out, value.astype(dtype), me, dim)
    for step in (1, 3, 2):
        got = shift(value, axis, step).astype(dtype)
        out = lax.dynamic_update_index_in_dim(out, got, (me - step) % 4, dim)
    return out


def reduce_zy(grads):
    return lax.psum_scatter(grads, ("z", "y"), scatter_dimension=0, tiled=True)


def exchange_zy(grads):
    parts = grads.reshape(16, 32, grads.shape[-1])
    parts = lax.all_to_all(parts, ("z", "y"), split_axis=0, concat_axis=0, tiled=True)
    return jnp.sum(parts.astype(F32), axis=0).astype(LOW)


def reduce_x_gather(part):
    half = part.shape[-1] // 2
    both = jnp.stack([part[:, :half], part[:, half:]], axis=0)
    mine = reduce_over(both.reshape(4, 16, half), "x", 0)
    xh = lax.axis_index("xh")
    other = lax.ppermute(mine, "xh", [(0, 1), (1, 0)])
    first = jnp.where(xh == 0, mine, other)
    second = jnp.where(xh == 0, other, mine)
    first = gather_over(first, "z", 0)
    second = gather_over(second, "y", 0)
    first = gather_over(first, "y", 0, F32).reshape(256, half)
    second = gather_over(second, "z", 1, F32).reshape(256, half)
    return jnp.concatenate([first, second], axis=1)


def gather_weight(shard):
    half = shard.shape[0] // 2
    up = x_shift(shard[:half], 1)
    down = x_shift(shard[half:], -1)
    return [shard, up, down, core_swap(shard), core_swap(up), core_swap(down)]


def dot_t(left, right):
    return lax.dot_general(left, right, (((1,), (1,)), ((), ())), preferred_element_type=F32)


def dot_n(left, right):
    return lax.dot_general(left, right, (((1,), (0,)), ((), ())), preferred_element_type=F32)


def dot_r(left, right):
    return lax.dot_general(left, right, (((0,), (0,)), ((), ())), preferred_element_type=F32)


def whole(shape):
    return pl.BlockSpec(shape, lambda *_: (0,) * len(shape))


def per_block(shape):
    return pl.BlockSpec((1,) + shape, lambda i: (i,) + (0,) * len(shape))


def smem():
    return pl.BlockSpec(memory_space=pltpu.SMEM)


def anywhere():
    return pl.BlockSpec(memory_space=pl.ANY)


def shaped(shape, dtype):
    return jax.ShapeDtypeStruct(shape, dtype)


def fetch(shards, pieces, full, sems):
    rows = pieces[0].shape[0]
    half = rows // 2
    at = [
        shards[0] * rows,
        shards[1] * rows,
        shards[1] * rows + half,
        shards[2] * rows,
        shards[3] * rows,
        shards[3] * rows + half,
    ]
    copies = []
    for n, (piece, where) in enumerate(zip(pieces, at)):
        where = pl.multiple_of(where, half)
        copy = pltpu.make_async_copy(
            piece, full.at[pl.ds(where, piece.shape[0]), :], sems.at[n]
        )
        copy.start()
        copies.append(copy)
    return copies


def fetch_feed(shards, pieces, w_out, w_gu, w_down, sems):
    groups = ([], [], [])
    n = 0
    for s in range(4):
        for part, (first, end) in enumerate(FEED_CUTS):
            piece = pieces[len(FEED_CUTS) * s + part]
            at = 0
            while first + at < end:
                block, off = divmod(first + at, 256)
                size = min(256 - off, end - first - at)
                src = piece.at[pl.ds(at, size), :]
                if block < 6:
                    where = pl.multiple_of(shards[s] * 256 + off, 128)
                    dst = w_gu.at[pl.ds(where, size), pl.ds(block * 1024, 1024)]
                    group = 1
                elif block < 8:
                    where = pl.multiple_of(shards[s] * 512 + (block - 6) * 256 + off, 128)
                    dst = w_out.at[pl.ds(where, size), :]
                    group = 0
                else:
                    where = pl.multiple_of(shards[s] * 768 + (block - 8) * 256 + off, 128)
                    dst = w_down.at[pl.ds(where, size), :]
                    group = 2
                groups[group].append(pltpu.make_async_copy(src, dst, sems.at[n]))
                n += 1
                at += size
    for group in groups:
        for copy in group:
            copy.start()
    return groups


def settle(copies):
    for copy in copies:
        copy.wait()


def scale_of(value):
    return lax.rsqrt(jnp.mean(value * value, axis=-1, keepdims=True) + EPSILON)


def turn(value):
    return jnp.concatenate([value[:, HEAD // 2 :], value[:, : HEAD // 2]], axis=1)


def project_kernel(
    shards, x_ref, gain_ref, gq_ref, gk_ref, cos_ref, sin_ref, *rest
):
    pieces, (q_ref, kv_ref, raw_ref, left_ref, w, sems) = rest[:6], rest[6:]
    copies = fetch(shards, pieces, w, sems)
    x = x_ref[...].astype(F32)
    h = (x * scale_of(x) * gain_ref[...]).astype(LOW)
    for f in range(4):
        left_ref[f % 2, :, (f // 2) * 256 : (f // 2) * 256 + 256] = h[:, f * 256 : f * 256 + 256]
    cosine, sine = cos_ref[...], sin_ref[...]
    settle(copies)
    for tile in range(8):
        product = dot_n(h, w[:, tile * 512 : tile * 512 + 512])
        for part in range(4):
            n = tile * 4 + part
            raw = product[:, part * HEAD : part * HEAD + HEAD]
            if n >= 24:
                kv_ref[n - 24, 1] = raw.astype(LOW)
                continue
            raw_ref[n] = raw
            gain = gq_ref[...] if n < 16 else gk_ref[...]
            u = raw * scale_of(raw) * gain
            u = (u * cosine + turn(u) * sine).astype(LOW)
            if n < 16:
                q_ref[n] = u
            else:
                kv_ref[n - 16, 0] = u


def project(shards, x, gain, gain_q, gain_k, cosine, sine, pieces):
    return pl.pallas_call(
        project_kernel,
        in_specs=[smem()] + [pl.BlockSpec(memory_space=pltpu.VMEM)] * 6 + [anywhere()] * 6,
        out_shape=[
            shaped((16, ROWS, HEAD), LOW),
            shaped((8, 2, ROWS, HEAD), LOW),
            shaped((24, ROWS, HEAD), F32),
            shaped((2, ROWS, 512), LOW),
        ],
        scratch_shapes=[pltpu.VMEM((1024, 4096), LOW), pltpu.SemaphoreType.DMA((6,))],
        compiler_params=pltpu.CompilerParams(vmem_limit_bytes=32 * 2**20),
        cost_estimate=pl.CostEstimate(
            flops=10**9, bytes_accessed=12 * 2**20, transcendentals=10**4
        ),
        name="project",
    )(shards, x, gain, gain_q, gain_k, cosine, sine, *pieces)


def feed_kernel(shards, o_ref, x_ref, cot_ref, gain_ref, *rest):
    (y_ref, mid_ref, left_ref, right_ref, do_ref, term_ref) = rest[16:22]
    (w_out, w_gu, w_down, merged, sems) = rest[22:]
    out_copies, gu_copies, down_copies = fetch_feed(shards, rest[:16], w_out, w_gu, w_down, sems)
    for n in range(16):
        merged[:, n * HEAD : n * HEAD + HEAD] = o_ref[n]
    for f in range(4):
        for g in range(2):
            at = f * 512 + g * 256
            left_ref[f % 2, 4 + g, :, (f // 2) * 256 : (f // 2) * 256 + 256] = merged[:, at : at + 256]
    cot = cot_ref[...]
    gain = gain_ref[...]
    settle(out_copies)
    middle = x_ref[...].astype(F32) + dot_n(merged[...], w_out[...])
    scale = scale_of(middle)
    normal = middle * scale
    h = (normal * gain).astype(LOW)
    for f in range(4):
        left_ref[f % 2, 0, :, (f // 2) * 256 : (f // 2) * 256 + 256] = h[:, f * 256 : f * 256 + 256]
    settle(gu_copies)
    settle(down_copies)
    total = middle
    dh = jnp.zeros_like(middle)
    for tile in range(6):
        at = tile * 512
        gate = dot_n(h, w_gu[:, at : at + 512])
        up = dot_n(h, w_gu[:, 3072 + at : 3072 + at + 512])
        sg = 1.0 / (1.0 + jnp.exp(-gate))
        swish = gate * sg
        hidden = (swish * up).astype(LOW)
        for part in range(2):
            f, g = divmod(tile * 2 + part, 3)
            left_ref[f % 2, 1 + g, :, (f // 2) * 256 : (f // 2) * 256 + 256] = hidden[
                :, part * 256 : part * 256 + 256
            ]
        total = total + dot_n(hidden, w_down[at : at + 512, :])
        dhidden = dot_t(cot, w_down[at : at + 512, :])
        dgate = (dhidden * up * sg * (1.0 + gate * (1.0 - sg))).astype(LOW)
        dup = (dhidden * swish).astype(LOW)
        right_ref[:, at : at + 512] = dgate
        right_ref[:, 3072 + at : 3072 + at + 512] = dup
        dh = dh + dot_t(dgate, w_gu[:, at : at + 512])
        dh = dh + dot_t(dup, w_gu[:, 3072 + at : 3072 + at + 512])
    y_ref[...] = total.astype(LOW)
    term_ref[...] = jnp.sum(dh * normal, axis=0, keepdims=True)
    dn = dh * gain
    dmid = cot.astype(F32) + scale * (dn - normal * jnp.mean(dn * normal, axis=-1, keepdims=True))
    mid_ref[...] = dmid
    da = dmid.astype(LOW)
    right_ref[:, 6144:7168] = cot
    right_ref[:, 7168:8192] = da
    for tile in range(4):
        back = dot_t(da, w_out[tile * 512 : tile * 512 + 512, :]).astype(LOW)
        for part in range(4):
            do_ref[tile * 4 + part] = back[:, part * HEAD : part * HEAD + HEAD]


def feed(shards, o, x, cot, gain, pieces):
    return pl.pallas_call(
        feed_kernel,
        in_specs=[smem()] + [pl.BlockSpec(memory_space=pltpu.VMEM)] * 4 + [anywhere()] * 16,
        out_shape=[
            shaped((ROWS, 1024), LOW),
            shaped((ROWS, 1024), F32),
            shaped((2, 6, ROWS, 512), LOW),
            shaped((ROWS, 8192), LOW),
            shaped((16, ROWS, HEAD), LOW),
            shaped((1, 1024), F32),
        ],
        scratch_shapes=[
            pltpu.VMEM((2048, 1024), LOW),
            pltpu.VMEM((1024, 6144), LOW),
            pltpu.VMEM((3072, 1024), LOW),
            pltpu.VMEM((ROWS, 2048), LOW),
            pltpu.SemaphoreType.DMA((52,)),
        ],
        compiler_params=pltpu.CompilerParams(vmem_limit_bytes=48 * 2**20),
        cost_estimate=pl.CostEstimate(
            flops=7 * 10**9, bytes_accessed=30 * 2**20, transcendentals=10**6
        ),
        name="feed",
    )(shards, o, x, cot, gain, *pieces)


def lay_left(left_t, half, left):
    columns = left.astype(F32).T.astype(LOW)
    for xl in range(2):
        for y in range(4):
            for z in range(4):
                to, at = ((z * 4 + y) * 2 + xl) * 16, ((xl * 4 + y) * 4 + z) * 16
                left_t[to : to + 16, half * ROWS : half * ROWS + ROWS] = columns[at : at + 16, :]


def weight_kernel(mine_ref, other_ref, right_ref, other_right_ref, out_ref, left_t, right):
    t = pl.program_id(0)

    @pl.when((t == 0) | (t >= 6))
    def _():
        lay_left(left_t, 0, mine_ref[0])
        lay_left(left_t, 1, other_ref[0])

    right[:ROWS, :] = right_ref[...]
    right[ROWS:, :] = other_right_ref[...]
    out_ref[...] = dot_n(left_t[...], right[...]).astype(LOW)


def feed_weight_grads(mine, other, right, other_right):
    def group(t):
        return jnp.maximum(t - 5, 0)

    def column(t):
        return jnp.where(t < 6, t, jnp.where(t < 9, 6, 7))

    left = pl.BlockSpec((1, ROWS, 512), lambda t: (group(t), 0, 0))
    wide = pl.BlockSpec((ROWS, 1024), lambda t: (0, column(t)))
    return pl.pallas_call(
        weight_kernel,
        grid=(11,),
        in_specs=[left, left, wide, wide],
        out_specs=pl.BlockSpec((512, 1024), lambda t: (0, t)),
        out_shape=shaped((512, 11264), LOW),
        scratch_shapes=[pltpu.VMEM((512, 2 * ROWS), LOW), pltpu.VMEM((2 * ROWS, 1024), LOW)],
        compiler_params=pltpu.CompilerParams(vmem_limit_bytes=16 * 2**20),
        cost_estimate=pl.CostEstimate(
            flops=3 * 10**9, bytes_accessed=16 * 2**20, transcendentals=0
        ),
        name="feed_weight_grads",
    )(mine, other, right, other_right)


def attention_weight_kernel(
    mine_ref, other_ref, right_ref, other_right_ref, term_ref, out_ref, left_t, right
):
    t = pl.program_id(0)

    @pl.when(t == 0)
    def _():
        lay_left(left_t, 0, mine_ref[...])
        lay_left(left_t, 1, other_ref[...])

    @pl.when(t < 16)
    def _():
        right[:ROWS, :] = right_ref[...]
        right[ROWS:, :] = other_right_ref[...]
        out_ref[...] = dot_n(left_t[...], right[...]).astype(LOW)

    @pl.when(t == 16)
    def _():
        out_ref[...] = jnp.zeros_like(out_ref)
        for xl in range(2):
            for z in range(2):
                at = (z * 8 + xl) * 16
                out_ref[at : at + 16, :HEAD] = term_ref[z * 16 : z * 16 + 16, :].astype(LOW)


def attention_weight_grads(mine, other, right, other_right, terms):
    wide = pl.BlockSpec((ROWS, 256), lambda t: (0, jnp.minimum(t, 15)))
    left = whole((ROWS, 512))
    return pl.pallas_call(
        attention_weight_kernel,
        grid=(17,),
        in_specs=[left, left, wide, wide, whole((32, HEAD))],
        out_specs=pl.BlockSpec((512, 256), lambda t: (0, t)),
        out_shape=shaped((512, 4352), LOW),
        scratch_shapes=[pltpu.VMEM((512, 2 * ROWS), LOW), pltpu.VMEM((2 * ROWS, 256), LOW)],
        compiler_params=pltpu.CompilerParams(vmem_limit_bytes=16 * 2**20),
        cost_estimate=pl.CostEstimate(flops=10**9, bytes_accessed=6 * 2**20, transcendentals=0),
        name="attention_weight_grads",
    )(mine, other, right, other_right, terms)


def tail_kernel(
    shards, back_ref, raw_ref, x_ref, mid_ref, gain_ref, gq_ref, gk_ref, cos_ref, sin_ref, *rest
):
    pieces, (grad_ref, right_ref, term_ref, w, sems) = rest[:6], rest[6:]
    copies = fetch(shards, pieces, w, sems)
    cosine, sine = cos_ref[...], sin_ref[...]
    term_ref[...] = jnp.zeros_like(term_ref)
    for heads, first, place, gain_ref_ in ((16, 0, 1024, gq_ref), (8, 16, 1152, gk_ref)):
        gain = gain_ref_[...]
        term = jnp.zeros((ROWS, HEAD), F32)
        for n in range(heads):
            grad = back_ref[n // 2, n % 2] if first == 0 else back_ref[n, 2]
            grad = grad.astype(F32)
            raw = raw_ref[first + n]
            scale = scale_of(raw)
            unit = raw * scale
            grad = grad * cosine - turn(grad) * sine
            term = term + grad * unit
            grad = grad * gain
            grad = scale * (grad - unit * jnp.mean(grad * unit, axis=-1, keepdims=True))
            at = (first + n) * HEAD
            right_ref[:, at : at + HEAD] = grad.astype(LOW)
        term_ref[:, place : place + HEAD] = jnp.sum(term, axis=0, keepdims=True)
    for n in range(8):
        at = 3072 + n * HEAD
        right_ref[:, at : at + HEAD] = back_ref[n, 3]
    x = x_ref[...].astype(F32)
    scale = scale_of(x)
    normal = x * scale
    settle(copies)
    dh = dot_t(right_ref[...], w[...])
    term_ref[:, :1024] = jnp.sum(dh * normal, axis=0, keepdims=True)
    dn = dh * gain_ref[...]
    grad_ref[...] = mid_ref[...] + scale * (
        dn - normal * jnp.mean(dn * normal, axis=-1, keepdims=True)
    )


def tail(shards, back, raw, x, mid, gain, gain_q, gain_k, cosine, sine, pieces):
    return pl.pallas_call(
        tail_kernel,
        in_specs=[smem()] + [pl.BlockSpec(memory_space=pltpu.VMEM)] * 9 + [anywhere()] * 6,
        out_shape=[
            shaped((ROWS, 1024), F32),
            shaped((ROWS, 4096), LOW),
            shaped((1, 1280), F32),
        ],
        scratch_shapes=[pltpu.VMEM((1024, 4096), LOW), pltpu.SemaphoreType.DMA((6,))],
        compiler_params=pltpu.CompilerParams(vmem_limit_bytes=32 * 2**20),
        cost_estimate=pl.CostEstimate(
            flops=10**9, bytes_accessed=12 * 2**20, transcendentals=10**4
        ),
        name="tail",
    )(shards, back, raw, x, mid, gain, gain_q, gain_k, cosine, sine, *pieces)


def visible(first_key, query_block, start):
    key = first_key + lax.broadcasted_iota(jnp.int32, (CHUNK, 2 * ROWS), 0)
    query = query_block * ROWS + (lax.broadcasted_iota(jnp.int32, (CHUNK, 2 * ROWS), 1) & (ROWS - 1))
    return (key <= query) & ((key >= start) | (query < start))


def block_of(info):
    i = pl.program_id(0)
    return (i // 2) * 8 + info[1] * 2 + i % 2


def columns_of(value):
    return value.astype(F32).T.astype(LOW)


def forward_kernel(info, q_ref, kv0, kv1, kv2, kv3, o_ref, ot_ref, l_ref, k_ref, v_ref, vt):
    block = block_of(info)
    start = info[0]
    last = block // (CHUNK // ROWS)

    @pl.when(pl.program_id(0) == 0)
    def _():
        for back, piece in enumerate((kv0, kv1, kv2, kv3)):
            owner = lax.rem(info[1] + 4 - back, 4)
            for z in range(4):
                at = pl.ds(pl.multiple_of((z * 4 + owner) * 256, 256), 256)
                k_ref[at, :] = piece[2 * z : 2 * z + 2, 0].reshape(256, HEAD)
                v_ref[at, :] = piece[2 * z : 2 * z + 2, 1].reshape(256, HEAD)
        for c in range(vt.shape[0]):
            vt[c] = columns_of(v_ref[c * CHUNK : (c + 1) * CHUNK, :])

    q = q_ref[0]

    def step(c, carry, masked):
        total, mixed = carry
        keys = k_ref[pl.ds(pl.multiple_of(c * CHUNK, CHUNK), CHUNK), :]
        p = jnp.exp2(dot_t(keys, q) * EXP_SCALE)
        if masked:
            p = jnp.where(visible(c * CHUNK, block, start), p, 0.0)
        total = total + jnp.sum(p.reshape(CHUNK // 8, 8, 2 * ROWS), axis=0)
        mixed = mixed + dot_n(vt[c], p.astype(LOW))
        return total, mixed

    carry = (jnp.zeros((8, 2 * ROWS), F32), jnp.zeros((HEAD, 2 * ROWS), F32))
    carry = step(last, carry, True)
    carry = lax.fori_loop(0, jnp.minimum(last, 1), lambda c, x: step(c, x, True), carry)
    carry = lax.fori_loop(1, last, lambda c, x: step(c, x, False), carry)
    total = jnp.sum(carry[0], axis=0, keepdims=True)
    mixed = carry[1] / total
    ot_ref[0] = mixed
    o_ref[0] = mixed.T.astype(LOW)
    l_ref[0] = jnp.log2(total)


def backward_kernel(
    info, q_ref, do_ref, ot_ref, l_ref, k_ref, v_ref, dq_ref, dkv_ref, kt, dk_acc, dv_acc
):
    i = pl.program_id(0)
    block = block_of(info)
    start = info[0]
    q = q_ref[0]
    do = do_ref[0]
    last = block // (CHUNK // ROWS)

    @pl.when(i == 0)
    def _():
        dk_acc[...] = jnp.zeros_like(dk_acc)
        dv_acc[...] = jnp.zeros_like(dv_acc)
        for c in range(kt.shape[0]):
            kt[c] = columns_of(k_ref[c * CHUNK : (c + 1) * CHUNK, :])

    delta = jnp.sum(do.astype(F32).T * ot_ref[0], axis=0, keepdims=True)
    logs = l_ref[0]

    def step(c, dqt, masked):
        at = pl.ds(pl.multiple_of(c * CHUNK, CHUNK), CHUNK)
        p = jnp.exp2(dot_t(k_ref[at, :], q) * EXP_SCALE - logs)
        if masked:
            p = jnp.where(visible(c * CHUNK, block, start), p, 0.0)
        dp = dot_t(v_ref[at, :], do)
        ds = (p * (dp - delta)).astype(LOW)
        dv_acc[at, :] += dot_n(p.astype(LOW), do)
        dk_acc[at, :] += dot_n(ds, q)
        return dqt + dot_n(kt[c], ds)

    dqt = step(last, jnp.zeros((HEAD, 2 * ROWS), F32), True)
    dqt = lax.fori_loop(0, jnp.minimum(last, 1), lambda c, x: step(c, x, True), dqt)
    dqt = lax.fori_loop(1, last, lambda c, x: step(c, x, False), dqt)
    dq_ref[0] = (dqt * SCORE_SCALE).T.astype(LOW)

    @pl.when(i == pl.num_programs(0) - 1)
    def _():
        for z in range(4):
            for y in range(4):
                at = (z * 4 + y) * 256
                part = (dk_acc[at : at + 256, :] * SCORE_SCALE).astype(LOW)
                dkv_ref[y, 2 * z : 2 * z + 2, 0] = part.reshape(2, ROWS, HEAD)
                part = dv_acc[at : at + 256, :].astype(LOW)
                dkv_ref[y, 2 * z : 2 * z + 2, 1] = part.reshape(2, ROWS, HEAD)


def attention_forward(info, q, pieces):
    length = 32 * ROWS
    return pl.pallas_call(
        forward_kernel,
        grid=(8,),
        in_specs=[smem(), per_block((2 * ROWS, HEAD))] + [whole((8, 2, ROWS, HEAD))] * 4,
        out_specs=[
            per_block((2 * ROWS, HEAD)),
            per_block((HEAD, 2 * ROWS)),
            per_block((1, 2 * ROWS)),
            whole((length, HEAD)),
            whole((length, HEAD)),
        ],
        out_shape=[
            shaped((8, 2 * ROWS, HEAD), LOW),
            shaped((8, HEAD, 2 * ROWS), F32),
            shaped((8, 1, 2 * ROWS), F32),
            shaped((length, HEAD), LOW),
            shaped((length, HEAD), LOW),
        ],
        scratch_shapes=[pltpu.VMEM((length // CHUNK, HEAD, CHUNK), LOW)],
        compiler_params=pltpu.CompilerParams(vmem_limit_bytes=32 * 2**20),
        cost_estimate=pl.CostEstimate(
            flops=3 * 10**9, bytes_accessed=7 * 2**20, transcendentals=5 * 10**6
        ),
        name="attention_forward",
    )(info, q, *pieces)


def attention_backward(info, q, do, ot, logs, k, v):
    length = k.shape[0]
    return pl.pallas_call(
        backward_kernel,
        grid=(8,),
        in_specs=[
            smem(),
            per_block((2 * ROWS, HEAD)),
            per_block((2 * ROWS, HEAD)),
            per_block((HEAD, 2 * ROWS)),
            per_block((1, 2 * ROWS)),
            whole((length, HEAD)),
            whole((length, HEAD)),
        ],
        out_specs=[per_block((2 * ROWS, HEAD)), whole((4, 8, 2, ROWS, HEAD))],
        out_shape=[
            shaped((8, 2 * ROWS, HEAD), LOW),
            shaped((4, 8, 2, ROWS, HEAD), LOW),
        ],
        scratch_shapes=[
            pltpu.VMEM((length // CHUNK, HEAD, CHUNK), LOW),
            pltpu.VMEM((length, HEAD), F32),
            pltpu.VMEM((length, HEAD), F32),
        ],
        compiler_params=pltpu.CompilerParams(vmem_limit_bytes=32 * 2**20),
        cost_estimate=pl.CostEstimate(
            flops=8 * 10**9, bytes_accessed=10 * 2**20, transcendentals=5 * 10**6
        ),
        name="attention_backward",
    )(info, q, do, ot, logs, k, v)


def rotary_tables(where_at):
    half = HEAD // 2
    frequency = THETA ** (-(jnp.arange(half, dtype=F32) * 2.0) / HEAD)
    angles = where_at.astype(F32)[:, None] * frequency[None, :]
    cosine, sine = jnp.cos(angles), jnp.sin(angles)
    return jnp.concatenate([cosine, cosine], axis=-1), jnp.concatenate([-sine, sine], axis=-1)


def exchange_heads(value):
    return lax.all_to_all(value, ("z", "xh"), split_axis=0, concat_axis=0, tiled=True)


def pack_feed(w_gate, w_up, w_out, w_down):
    blocks = [w[:, n * 1024 : n * 1024 + 1024] for w in (w_gate, w_up) for n in range(3)]
    blocks += [w[n : n + 256] for w in (w_out, w_down) for n in range(0, w.shape[0], 256)]
    parts = []
    for first, end in FEED_CUTS:
        rows = []
        while first < end:
            block, off = divmod(first, 256)
            size = min(256 - off, end - first)
            rows.append(blocks[block][off : off + size])
            first += size
        parts.append(jnp.concatenate(rows, axis=0))
    return parts


def x_pair(value):
    return lax.ppermute(value, "xl", [(0, 1), (1, 0)])


def local(
    tokens,
    positions,
    attn_gain,
    w_query,
    w_key,
    w_value,
    query_gain,
    key_gain,
    w_out,
    ffn_gain,
    w_gate,
    w_up,
    w_down,
    cotangent,
):
    xl = lax.axis_index("xl")
    co = lax.axis_index("co")
    y = lax.axis_index("y")
    block = lax.axis_index("z") * 8 + y * 2 + lax.axis_index("xh")
    shard = xl * 2 + co
    shards = jnp.stack([shard, 2 * (1 - xl) + co, 2 * xl + 1 - co, 2 * (1 - xl) + 1 - co])
    shards = shards.astype(jnp.int32)

    qkv_pieces = gather_weight(jnp.concatenate([w_query, w_key, w_value], axis=1))

    gains = jnp.concatenate([attn_gain, ffn_gain, query_gain, key_gain])
    gains = jnp.concatenate([gains, jnp.zeros((1024 - 576,), LOW)]).reshape(1, 8, 128)
    pair = jnp.concatenate([gains, x_pair(gains)], axis=0)
    pair = jnp.where(xl == 0, pair, pair[::-1])
    swapped = core_swap(pair)
    quad = jnp.where(co == 0, jnp.stack([pair, swapped], 1), jnp.stack([swapped, pair], 1))
    quad = quad.reshape(4, 1024).astype(F32)
    gain_one = quad[:, :256].reshape(1, 1024)
    gain_two = quad[:, 256:512].reshape(1, 1024)
    gain_query = quad[:, 512:544].reshape(1, 128)
    gain_key = quad[:, 544:576].reshape(1, 128)

    packed = pack_feed(w_gate, w_up, w_out, w_down)
    feed_across = [x_shift(packed[0], 1), x_shift(packed[1], -1)]

    start = block * ROWS + ROWS - 1 - positions[ROWS - 1]
    info = jnp.stack([start, y]).astype(jnp.int32)
    cosine, sine = rotary_tables(positions)
    query, kv_send, raw, left_one = project(
        shards, tokens, gain_one, gain_query, gain_key, cosine, sine, qkv_pieces
    )

    heads_send = jnp.concatenate([query.reshape(8, 2, ROWS, HEAD), kv_send], axis=1)
    heads_send, feed_across[0], feed_across[1] = lax.optimization_barrier(
        (heads_send, feed_across[0], feed_across[1])
    )
    heads = exchange_heads(heads_send)
    heads, packed[2], packed[3] = lax.optimization_barrier((heads, packed[2], packed[3]))
    kv = heads[:, 2:]
    q_all = heads[:, :2].reshape(8, 2 * ROWS, HEAD)
    kv_pieces = [kv, shift(kv, "y", 1), shift(kv, "y", 2), shift(kv, "y", 3)]
    feed_across += [x_shift(packed[2], 1), x_shift(packed[3], -1)]
    o_send, mixed_t, logs, k_all, v_all = attention_forward(info, q_all, kv_pieces)
    o_send, feed_across[2], feed_across[3] = lax.optimization_barrier(
        (o_send, feed_across[2], feed_across[3])
    )
    feed_pieces = packed + feed_across
    feed_pieces = feed_pieces + [core_swap(piece) for piece in feed_pieces]
    merged = exchange_heads(o_send).reshape(16, ROWS, HEAD)

    output, grad_middle, lefts, right, grad_merged, gain_two_term = feed(
        shards, merged, tokens, cotangent, gain_two, feed_pieces
    )

    feed_part = feed_weight_grads(
        pick(lefts, co, 0), core_swap(pick(lefts, 1 - co, 0)), right, core_swap(right)
    )

    do_all = exchange_heads(grad_merged.reshape(8, 2 * ROWS, HEAD))
    do_all, feed_part = lax.optimization_barrier((do_all, feed_part))
    feed_part = reduce_zy(feed_part)
    dq_all, dkv_all = attention_backward(info, q_all, do_all, mixed_t, logs, k_all, v_all)
    dkv = reduce_over(dkv_all, "y", 0)
    back = exchange_heads(jnp.concatenate([dq_all.reshape(8, 2, ROWS, HEAD), dkv], axis=1))

    grad_tokens, attention_grads, terms = tail(
        shards,
        back,
        raw,
        tokens,
        grad_middle,
        gain_one,
        gain_query,
        gain_key,
        cosine,
        sine,
        qkv_pieces,
    )
    terms = jnp.concatenate([terms[:, :1024], gain_two_term, terms[:, 1024:]], axis=1)
    terms = jnp.pad(terms.reshape(18, 128), ((0, 14), (0, 0)))
    terms = terms + core_swap(terms)
    attention_part = attention_weight_grads(
        pick(left_one, co, 0),
        core_swap(pick(left_one, 1 - co, 0)),
        attention_grads,
        core_swap(attention_grads),
        terms,
    )
    attention_part, feed_part = lax.optimization_barrier((attention_part, feed_part))
    attention_part = exchange_zy(attention_part)
    feed_sum = reduce_x_gather(feed_part)
    wide = reduce_x_gather(attention_part)
    grad_down = jnp.concatenate(
        [feed_sum[:, 6144 + 1024 * g : 7168 + 1024 * g] for g in range(3)], axis=0
    )
    grad_out = jnp.concatenate(
        [feed_sum[:, 9216 + 1024 * g : 10240 + 1024 * g] for g in range(2)], axis=0
    )
    gain_all = wide[:18, 4096:4224].reshape(2304)
    return (
        output,
        grad_tokens,
        lax.dynamic_slice_in_dim(gain_all, shard * 256, 256),
        wide[:, :2048],
        wide[:, 2048:3072],
        wide[:, 3072:4096],
        lax.dynamic_slice_in_dim(gain_all, 2048 + shard * 32, 32),
        lax.dynamic_slice_in_dim(gain_all, 2176 + shard * 32, 32),
        grad_out,
        lax.dynamic_slice_in_dim(gain_all, 1024 + shard * 256, 256),
        feed_sum[:, :3072],
        feed_sum[:, 3072:6144],
        grad_down,
    )


def solution(mesh):
    axes = ("xl", "co", "z", "y", "xh")
    fine = Mesh(mesh.devices.reshape(2, 2, 4, 4, 2), axes)
    rows = P(axes, None)
    shard = P(("xl", "co"), None)
    vector = P(("xl", "co"))
    in_specs = (
        rows,
        P(axes),
        vector,
        shard,
        shard,
        shard,
        vector,
        vector,
        shard,
        vector,
        shard,
        shard,
        shard,
        rows,
    )
    out_specs = (
        rows,
        rows,
        vector,
        shard,
        shard,
        shard,
        vector,
        vector,
        shard,
        vector,
        shard,
        shard,
        shard,
    )
    return jax.shard_map(local, mesh=fine, in_specs=in_specs, out_specs=out_specs, check_vma=False)
```

time: 711 us -> 555 us (0.78)
  local copies, waits for them, and re-layouts: 190 us -> 58.8 us
  matrix products: 65.3 us -> 0 us
  Pallas kernels: 34.7 us -> 92 us
  starting transfers between devices: 161 us -> 113 us
  other arithmetic: 59 us -> 21.2 us
  waiting for transfers between devices: 186 us -> 220 us
  blocking collectives: 0 us -> 23.7 us
  between operations: 3.22 us -> 16.2 us
    dot_general x15 -> x0, matrix products: 65.3 us -> none  [the longest x4 23.3 us: dot_t(): lax.dot_general(left, right, (((1,), (1,)), ((), ())), preferred_element_...]
    pallas_call x0 -> x5, Pallas kernels: none -> 54.6 us  [the longest x1 20 us: feed(): pl.pallas_call(feed_kernel, in_specs=[smem()] + [pl.BlockSpec(memory_spac...]
    dynamic_update_slice x24 -> x0, local copies, waits for them, and re-layouts: 49.7 us -> none  [gather_weight(): out = lax.dynamic_update_slice_in_dim(out, piece, at, 0)]
    ppermute x14 -> x12, waiting for transfers between devices: 5.63 us -> 34.1 us  [x_shift(): return lax.ppermute(value, ('xl', 'xh'), pairs)]
    all_to_all x0 -> x1, blocking collectives: none -> 23.7 us  [exchange_heads(): lax.all_to_all(value, ('z', 'xh'), split_axis=0, concat_axis=0, tiled=True)]
    reshape x15 -> x2, local copies, waits for them, and re-layouts: 22.7 us -> 0.85 us  [the longest x1 0.77 us: local(): gain_key = quad[:, 544:576].reshape(1, 128)]
    all_to_all x5 -> x3, starting transfers between devices: 31.3 us -> 14 us  [exchange_heads(): lax.all_to_all(value, ('z', 'xh'), split_axis=0, concat_axis=0, tiled=True)]
    all_to_all x5 -> x3, waiting for transfers between devices: 10.2 us -> 25.9 us  [exchange_heads(): lax.all_to_all(value, ('z', 'xh'), split_axis=0, concat_axis=0, tiled=True)]
  transfers between devices with their start and end apart: 94 -> 67, of which waited for: 38 -> 28; matrix products, arithmetic and copies ran while one was open for 42% -> 7% of each run, Pallas kernels for 5% -> 13%
where the time goes in v2:
time: 555 us; the launch traced here: 544 us
  waiting for transfers between devices  220 us (40%)
  starting transfers between devices  113 us (20%)
  Pallas kernels  92 us (17%)
  local copies, waits for them, and re-layouts  58.8 us (11%)
  blocking collectives  23.7 us (4%)
  other arithmetic  21.2 us (4%)
  between operations  16.2 us (3%)
    ppermute x30, waiting for transfers between devices, shift(): return lax.ppermute(value, axis, [(i, (i + step) % 4) for i in range(4)])  144 us
    ppermute x30, starting transfers between devices, shift(): return lax.ppermute(value, axis, [(i, (i + step) % 4) for i in range(4)])  66 us
    unnamed x110, local copies, waits for them, and re-layouts  35.2 us
    ppermute x12, waiting for transfers between devices, x_shift(): return lax.ppermute(value, ('xl', 'xh'), pairs)  34.1 us
    all_to_all x3, waiting for transfers between devices, exchange_heads(): lax.all_to_all(value, ('z', 'xh'), split_axis=0, concat_axis=0, tiled=True)  25.9 us
    all_to_all x1, blocking collectives, exchange_heads(): lax.all_to_all(value, ('z', 'xh'), split_axis=0, concat_axis=0, tiled=True)  23.7 us
    pallas_call x1, Pallas kernels, feed(): pl.pallas_call(feed_kernel, in_specs=[smem()] + [pl.BlockSpec(memory_spac...  20 us
    pallas_call x1, Pallas kernels, attention_backward(): pl.pallas_call(backward_kernel, grid=(8,), in_specs=[smem(), per_block((2...  19.6 us
  transfers between devices with their start and end apart: 67, of which 28 were waited for; matrix products, arithmetic and copies ran while one was open for 7% of the time, Pallas kernels for 13%

profile of v2, /device:TPU:0, one launch (start us, length us, event | category | flops | bytes accessed | tf_op | source)
XLA Modules:
  0.0 544.5 jit_solution(8006163464799528856)
XLA Ops:
  21.9 19.7 %collective-permute-done.2.rest_1_ = bf16[128,4096]{1,0:T(8,128)(2,1)S(1)} collective-permute-done((bf16[128,4096]{1,0:T(8,128)(2,1)}, bf16[128,4096]{1,0:T(8,128)(2,1)S(1)}, u32[]{:S(2)}, u32[]{:S(2)}) %collective-permute-start.2) | collective-permute-done | bytes 1048608 | tf_op jit(solution)/shard_map/ppermute | solution.py:27
  48.1 5.7 %project.1 = (bf16[16,128,128]{2,1,0:T(8,128)(2,1)S(1)}, bf16[8,2,128,128]{3,2,1,0:T(8,128)(2,1)S(1)}, f32[24,128,128]{2,1,0:T(8,128)S(1)}, bf16[2,128,512]{2,1,0:T(8,128)(2,1)S(1)}) custom-call(s32[4]{0:T(128)S(1)} %pad_add_fusion.1.shards, bf16[128,1024]{1,0:T(8,128)(2,1)S(1)} %copy-done.7, f32[1,1024]{1,0:T(1,128)S(1)} %bitcast.186, ...), custom_call_target="tpu_custom_call" | custom-call | flops 1000000000 | bytes 12582912 | tf_op jit(solution)/shard_map/project/pallas_call | solution.py:239
  56.0 4.4 collective-permute-done.7.rest_4_
  60.4 5.7 %all-to-all-start = ((bf16[8,4,128,128]{3,2,1,0:T(8,128)(2,1)}), bf16[8,4,128,128]{3,2,1,0:T(8,128)(2,1)}, u32[]{:S(2)}, u32[]{:S(2)}) async-start(bf16[8,4,128,128]{3,2,1,0:T(8,128)(2,1)} %pad_maximum_fusion.5), calls=%async_computation | async-start | bytes 2097152 | tf_op jit(solution)/shard_map/all_to_all | solution.py:655
  69.4 13.8 %all-to-all-done = bf16[8,4,128,128]{3,2,1,0:T(8,128)(2,1)} async-done(((bf16[8,4,128,128]{3,2,1,0:T(8,128)(2,1)}), bf16[8,4,128,128]{3,2,1,0:T(8,128)(2,1)}, u32[]{:S(2)}, u32[]{:S(2)}) %all-to-all-start) | async-done | bytes 1048608 | tf_op jit(solution)/shard_map/all_to_all | solution.py:655
  95.3 10.2 %collective-permute-done.10.kv2 = bf16[8,2,128,128]{3,2,1,0:T(8,128)(2,1)} collective-permute-done((bf16[8,2,128,128]{3,2,1,0:T(8,128)(2,1)}, bf16[8,2,128,128]{3,2,1,0:T(8,128)(2,1)}, u32[]{:S(2)}, u32[]{:S(2)}) %collective-permute-start.10) | collective-permute-done | bytes 524320 | tf_op jit(solution)/shard_map/ppermute | solution.py:33
  105.5 8.0 %collective-permute-done.11.kv3 = bf16[8,2,128,128]{3,2,1,0:T(8,128)(2,1)} collective-permute-done((bf16[8,2,128,128]{3,2,1,0:T(8,128)(2,1)}, bf16[8,2,128,128]{3,2,1,0:T(8,128)(2,1)}, u32[]{:S(2)}, u32[]{:S(2)}) %collective-permute-start.11) | collective-permute-done | bytes 524320 | tf_op jit(solution)/shard_map/ppermute | solution.py:33
  114.6 17.8 %attention_forward.1 = (bf16[8,256,128]{2,1,0:T(8,128)(2,1)S(1)}, f32[8,128,256]{2,1,0:T(8,128)S(1)}, f32[8,1,256]{2,1,0:T(1,128)S(1)}, bf16[4096,128]{1,0:T(8,128)(2,1)S(1)}, bf16[4096,128]{1,0:T(8,128)(2,1)S(1)}) custom-call(s32[2]{0:T(128)S(1)} %pad_add_fusion.2.info, bf16[8,256,128]{2,1,0:T(8,128)(2,1)S(1)} %bitcast.182, ...), custom_call_target="tpu_custom_call" | custom-call | flops 3000000000 | bytes 7340032 | tf_op jit(solution)/shard_map/attention_forward/pallas_call | solution.py:587
  138.2 4.9 collective-permute-done.15.rest_9_
  150.3 4.1 all-to-all-start.1
  154.6 12.1 %all-to-all-done.1 = bf16[8,256,128]{2,1,0:T(8,128)(2,1)} async-done(((bf16[8,256,128]{2,1,0:T(8,128)(2,1)}), bf16[8,256,128]{2,1,0:T(8,128)(2,1)}, u32[]{:S(2)}, u32[]{:S(2)}) %all-to-all-start.1) | async-done | bytes 524320 | tf_op jit(solution)/shard_map/all_to_all | solution.py:655
  171.8 20.0 %feed.1 = (bf16[128,1024]{1,0:T(8,128)(2,1)}, f32[128,1024]{1,0:T(8,128)S(1)}, bf16[2,6,128,512]{3,2,1,0:T(8,128)(2,1)}, bf16[128,8192]{1,0:T(8,128)(2,1)}, bf16...) custom-call(s32[4]{0:T(128)S(1)} %pad_add_fusion.1.shards, bf16[16,128,128]{2,1,0:T(8,128)(2,1)} %bitcast.12.o_ref, ...), custom_call_target="tpu_custom_call" | custom-call | flops 7000000000 | bytes 31457280 | tf_op jit(solution)/shard_map/feed/pallas_call | solution.py:315
  196.5 4.1 all-to-all-start.2
  203.6 9.5 %feed_weight_grads.1 = bf16[512,11264]{1,0:T(8,128)(2,1)S(1)} custom-call(bf16[6,128,512]{2,1,0:T(8,128)(2,1)S(1)} %copy-done.2, bf16[6,128,512]{2,1,0:T(8,128)(2,1)} %collective-permute-done.22.other_ref, bf16[128,8192]{1,0:T(8,128)(2,1)S(1)} %copy-done.3, bf16[128,8192]{1,0:T(8,128)(2,1)} %collective-permute-done.23.other_right_ref), custom_call_target="tpu_custom_call" | custom-call | flops 3000000000 | bytes 16777216 | tf_op jit(solution)/shard_map/feed_weight_grads/pallas_call | solution.py:372
  213.1 4.1 copy-done
  223.3 19.6 %attention_backward.1 = (bf16[8,256,128]{2,1,0:T(8,128)(2,1)S(1)}, bf16[4,8,2,128,128]{4,3,2,1,0:T(8,128)(2,1)S(1)}) custom-call(s32[2]{0:T(128)S(1)} %copy-done.32, bf16[8,256,128]{2,1,0:T(8,128)(2,1)S(1)} %bitcast.183, bf16[8,256,128]{2,1,0:T(8,128)(2,1)} %all-to-all-done.2.do_ref, f32[8,128,256]{2,1,0:T(8,128)S(1)} %copy-done.34, ...), custom_call_target="tpu_custom_call" | custom-call | flops 8000000000 | bytes 10485760 | tf_op jit(solution)/shard_map/attention_backward/pallas_call | solution.py:616
  247.0 8.6 %collective-permute-start.25 = (bf16[8,2,128,128]{3,2,1,0:T(8,128)(2,1)}, bf16[8,2,128,128]{3,2,1,0:T(8,128)(2,1)}, u32[]{:S(2)}, u32[]{:S(2)}) collective-permute-start(bf16[8,2,128,128]{3,2,1,0:T(8,128)(2,1)} %get-tuple-element.98), channel_id=1, source_target_pairs={{0,6},{2,0},{4,2},{6,4},{1,7},{3,1},{5,3},{7,5},{8,14},{10,8},{12,... | collective-permute-start | bytes 1572872 | tf_op jit(solution)/shard_map/ppermute | solution.py:33
  257.6 24.1 %collective-permute-done.24 = bf16[8,2,128,128]{3,2,1,0:T(8,128)(2,1)} collective-permute-done((bf16[8,2,128,128]{3,2,1,0:T(8,128)(2,1)}, bf16[8,2,128,128]{3,2,1,0:T(8,128)(2,1)}, u32[]{:S(2)}, u32[]{:S(2)}) %collective-permute-start.24) | collective-permute-done | bytes 524320 | tf_op jit(solution)/shard_map/ppermute | solution.py:33
  281.7 13.5 %collective-permute-done.26 = bf16[8,2,128,128]{3,2,1,0:T(8,128)(2,1)} collective-permute-done((bf16[8,2,128,128]{3,2,1,0:T(8,128)(2,1)}, bf16[8,2,128,128]{3,2,1,0:T(8,128)(2,1)}, u32[]{:S(2)}, u32[]{:S(2)}) %collective-permute-start.26) | collective-permute-done | bytes 524320 | tf_op jit(solution)/shard_map/ppermute | solution.py:33
  297.3 23.7 %all_to_all.25.back_ref = bf16[8,4,128,128]{3,2,1,0:T(8,128)(2,1)S(1)} all-to-all(bf16[8,4,128,128]{3,2,1,0:T(8,128)(2,1)S(1)} %pad_maximum_fusion.6), channel_id=1, replica_groups=mesh['xl'=2,'co'=2,'z'=4,'y'=4,'xh'=2] {'z','xh'}, dimensions={0} | all-to-all | bytes 2097152 | tf_op jit(solution)/shard_map/all_to_all | solution.py:655
  321.0 10.1 %tail.1 = (f32[128,1024]{1,0:T(8,128)}, bf16[128,4096]{1,0:T(8,128)(2,1)}, f32[1,1280]{1,0:T(1,128)S(1)}) custom-call(s32[4]{0:T(128)S(1)} %pad_add_fusion.1.shards, bf16[8,4,128,128]{3,2,1,0:T(8,128)(2,1)S(1)} %all_to_all.25.back_ref, f32[24,128,128]{2,1,0:T(8,128)S(1)} %copy-done.6, bf16[128,1024]{1,0:T(8,128)(2,1)S(1)} %copy-done.7, ...), custom_call_target="tpu_custom_call" | custom-call | flops 1000000000 | bytes 12582912 | tf_op jit(solution)/shard_map/tail/pallas_call | solution.py:467
  335.0 9.3 %attention_weight_grads.1 = bf16[512,4352]{1,0:T(8,128)(2,1)S(1)} custom-call(bf16[128,512]{1,0:T(8,128)(2,1)S(1)} %get-tuple-element.120.mine_ref, bf16[128,512]{1,0:T(8,128)(2,1)S(1)} %collective-permute-done.27.other_ref, bf16[128,4096]{1,0:T(8,128)(2,1)} %get-tuple-element.73.right_ref, bf16[128,4096]{1,0:T(8,128)(2,1)S(1)} %collective-permute-done.28.other_right_ref, ...), custom_call_target="tpu_custom_call" | custom-call | flops 1000000000 | bytes 6291456 | tf_op jit(solution)/shard_map/attention_weight_grads/pallas_call | solution.py:415
  351.4 8.0 %collective-permute-done.46 = bf16[16,5632]{1,0:T(8,128)(2,1)S(1)} collective-permute-done((bf16[16,5632]{1,0:T(8,128)(2,1)S(1)}, bf16[16,5632]{1,0:T(8,128)(2,1)S(1)}, u32[]{:S(2)}, u32[]{:S(2)}) %collective-permute-start.46) | collective-permute-done | bytes 180256 | tf_op jit(solution)/shard_map/ppermute | solution.py:27
  361.2 7.8 %all-to-all-start.4 = ((bf16[16,32,4352]{2,1,0:T(8,128)(2,1)}), bf16[16,32,4352]{2,1,0:T(8,128)(2,1)}, u32[]{:S(2)}, u32[]{:S(2)}) async-start(bf16[16,32,4352]{2,1,0:T(8,128)(2,1)} %bitcast.180), calls=%async_computation.5 | async-start | bytes 8912896 | tf_op jit(solution)/shard_map/all_to_all | solution.py:84
  378.1 54.3 %collective-permute-done.50 = bf16[16,5632]{1,0:T(8,128)(2,1)S(1)} collective-permute-done((bf16[16,5632]{1,0:T(8,128)(2,1)S(1)}, bf16[16,5632]{1,0:T(8,128)(2,1)S(1)}, u32[]{:S(2)}, u32[]{:S(2)}) %collective-permute-start.50) | collective-permute-done | bytes 180256 | tf_op jit(solution)/shard_map/ppermute | solution.py:33
  450.9 9.8 %collective-permute-done.53 = bf16[4,16,5632]{2,1,0:T(8,128)(2,1)S(1)} collective-permute-done((bf16[4,16,5632]{2,1,0:T(8,128)(2,1)S(1)}, bf16[4,16,5632]{2,1,0:T(8,128)(2,1)S(1)}, u32[]{:S(2)}, u32[]{:S(2)}) %collective-permute-start.53) | collective-permute-done | bytes 720928 | tf_op jit(solution)/shard_map/ppermute | solution.py:33
  463.0 9.5 %collective-permute-done.54 = bf16[4,16,5632]{2,1,0:T(8,128)(2,1)S(1)} collective-permute-done((bf16[4,16,5632]{2,1,0:T(8,128)(2,1)S(1)}, bf16[4,16,5632]{2,1,0:T(8,128)(2,1)S(1)}, u32[]{:S(2)}, u32[]{:S(2)}) %collective-permute-start.54) | collective-permute-done | bytes 720928 | tf_op jit(solution)/shard_map/ppermute | solution.py:33
  473.4 4.2 collective-permute-done.59
  479.9 3.3 pad_maximum_fusion
  489.8 3.6 pad_maximum_fusion.1
  501.3 5.6 %collective-permute-start.40 = (bf16[16,2176]{1,0:T(8,128)(2,1)S(1)}, bf16[16,2176]{1,0:T(8,128)(2,1)S(1)}, u32[]{:S(2)}, u32[]{:S(2)}) collective-permute-start(bf16[16,2176]{1,0:T(8,128)(2,1)S(1)} %get-tuple-element.84), channel_id=1, source_target_pairs={{0,8},{8,16},{16,24},{24,0},{1,9},{9,17},{17,25},{25,1},{2,10},{10... | collective-permute-start | bytes 208904 | tf_op jit(solution)/shard_map/ppermute | solution.py:33
  506.9 4.5 collective-permute-start.42
  (315 shorter events, 164.5 us)
Async XLA Ops:
  10.0 32.0 %collective-permute-start = (bf16[1,8,128]{2,1,0:T(8,128)(2,1)S(1)}, bf16[1,8,128]{2,1,0:T(8,128)(2,1)S(1)}, u32[]{:S(2)}, u32[]{:S(2)}) collective-permute-start(bf16[1,8,128]{2,1,0:T(8,128)(2,1)S(1)} %bitcast.205), channel_id=1, source_target_pairs={{0,64},{64,0},{1,65},{65,1},{2,66},{66,2},{3,67},{67,3},{4,68},{68... | collective-permute-start | bytes 6152 | tf_op jit(solution)/shard_map/ppermute | solution.py:674
  13.0 35.0 %collective-permute-start.4 = (bf16[256,4096]{1,0:T(8,128)(2,1)S(1)}, bf16[256,4096]{1,0:T(8,128)(2,1)}, u32[]{:S(2)}, u32[]{:S(2)}) collective-permute-start(bf16[256,4096]{1,0:T(8,128)(2,1)S(1)} %constant_dynamic-update-slice_fusion.rest_0_), channel_id=1, source_target_pairs={{0,32},{32,0},{1,33},{33,1},{2,34},{34,2},{3,35},{35,3},{4,36},{36... | collective-permute-start | bytes 6291464 | tf_op jit(solution)/shard_map/ppermute | solution.py:37
  14.6 27.0 %collective-permute-start.2 = (bf16[128,4096]{1,0:T(8,128)(2,1)}, bf16[128,4096]{1,0:T(8,128)(2,1)S(1)}, u32[]{:S(2)}, u32[]{:S(2)}) collective-permute-start(bf16[128,4096]{1,0:T(8,128)(2,1)} %get-tuple-element.100), channel_id=1, source_target_pairs={{0,64},{64,1},{1,65},{65,0},{2,66},{66,3},{3,67},{67,2},{4,68},{68... | collective-permute-start | bytes 3145736 | tf_op jit(solution)/shard_map/ppermute | solution.py:27
  15.0 26.6 %collective-permute-start.3 = (bf16[128,4096]{1,0:T(8,128)(2,1)}, bf16[128,4096]{1,0:T(8,128)(2,1)}, u32[]{:S(2)}, u32[]{:S(2)}) collective-permute-start(bf16[128,4096]{1,0:T(8,128)(2,1)} %get-tuple-element.99), channel_id=1, source_target_pairs={{0,65},{64,0},{1,64},{65,1},{2,67},{66,2},{3,66},{67,3},{4,69},{68... | collective-permute-start | bytes 3145736 | tf_op jit(solution)/shard_map/ppermute | solution.py:27
  20.5 35.5 %collective-permute-start.8 = (bf16[256,1024]{1,0:T(8,128)(2,1)}, bf16[256,1024]{1,0:T(8,128)(2,1)}, u32[]{:S(2)}, u32[]{:S(2)}) collective-permute-start(bf16[256,1024]{1,0:T(8,128)(2,1)} %pad_maximum_fusion.8.rest_1_), channel_id=1, source_target_pairs={{0,65},{64,0},{1,64},{65,1},{2,67},{66,2},{3,66},{67,3},{4,69},{68... | collective-permute-start | bytes 1572872 | tf_op jit(solution)/shard_map/ppermute | solution.py:27
  60.4 22.8 %all-to-all-start = ((bf16[8,4,128,128]{3,2,1,0:T(8,128)(2,1)}), bf16[8,4,128,128]{3,2,1,0:T(8,128)(2,1)}, u32[]{:S(2)}, u32[]{:S(2)}) async-start(bf16[8,4,128,128]{3,2,1,0:T(8,128)(2,1)} %pad_maximum_fusion.5), calls=%async_computation | async-start | bytes 2097152 | tf_op jit(solution)/shard_map/all_to_all | solution.py:655
  83.2 53.5 %collective-permute-start.12 = (bf16[1152,1024]{1,0:T(8,128)(2,1)}, bf16[1152,1024]{1,0:T(8,128)(2,1)}, u32[]{:S(2)}, u32[]{:S(2)}) collective-permute-start(bf16[1152,1024]{1,0:T(8,128)(2,1)} %copy-done.46), channel_id=1, source_target_pairs={{0,64},{64,1},{1,65},{65,0},{2,66},{66,3},{3,67},{67,2},{4,68},{68... | collective-permute-start | bytes 7077896 | tf_op jit(solution)/shard_map/ppermute | solution.py:27
  84.8 51.9 %collective-permute-start.13 = (bf16[1152,1024]{1,0:T(8,128)(2,1)}, bf16[1152,1024]{1,0:T(8,128)(2,1)}, u32[]{:S(2)}, u32[]{:S(2)}) collective-permute-start(bf16[1152,1024]{1,0:T(8,128)(2,1)} %pad_maximum_fusion.2.rest_3_), channel_id=1, source_target_pairs={{0,65},{64,0},{1,64},{65,1},{2,67},{66,2},{3,66},{67,3},{4,69},{68... | collective-permute-start | bytes 7077896 | tf_op jit(solution)/shard_map/ppermute | solution.py:27
  88.7 16.7 %collective-permute-start.10 = (bf16[8,2,128,128]{3,2,1,0:T(8,128)(2,1)}, bf16[8,2,128,128]{3,2,1,0:T(8,128)(2,1)}, u32[]{:S(2)}, u32[]{:S(2)}) collective-permute-start(bf16[8,2,128,128]{3,2,1,0:T(8,128)(2,1)} %get-tuple-element.107.kv0), channel_id=1, source_target_pairs={{0,4},{2,6},{4,0},{6,2},{1,5},{3,7},{5,1},{7,3},{8,12},{10,14},{12... | collective-permute-start | bytes 1572872 | tf_op jit(solution)/shard_map/ppermute | solution.py:33
  91.9 21.6 %collective-permute-start.11 = (bf16[8,2,128,128]{3,2,1,0:T(8,128)(2,1)}, bf16[8,2,128,128]{3,2,1,0:T(8,128)(2,1)}, u32[]{:S(2)}, u32[]{:S(2)}) collective-permute-start(bf16[8,2,128,128]{3,2,1,0:T(8,128)(2,1)} %get-tuple-element.107.kv0), channel_id=1, source_target_pairs={{0,6},{2,0},{4,2},{6,4},{1,7},{3,1},{5,3},{7,5},{8,14},{10,8},{12,... | collective-permute-start | bytes 1572872 | tf_op jit(solution)/shard_map/ppermute | solution.py:33
  93.0 20.5 %collective-permute-start.9 = (bf16[8,2,128,128]{3,2,1,0:T(8,128)(2,1)}, bf16[8,2,128,128]{3,2,1,0:T(8,128)(2,1)}, u32[]{:S(2)}, u32[]{:S(2)}) collective-permute-start(bf16[8,2,128,128]{3,2,1,0:T(8,128)(2,1)} %get-tuple-element.107.kv0), channel_id=1, source_target_pairs={{0,2},{2,4},{4,6},{6,0},{1,3},{3,5},{5,7},{7,1},{8,10},{10,12},{12... | collective-permute-start | bytes 1572872 | tf_op jit(solution)/shard_map/ppermute | solution.py:33
  105.5 49.1 %collective-permute-start.16 = (bf16[1152,1024]{1,0:T(8,128)(2,1)}, bf16[1152,1024]{1,0:T(8,128)(2,1)}, u32[]{:S(2)}, u32[]{:S(2)}) collective-permute-start(bf16[1152,1024]{1,0:T(8,128)(2,1)} %copy-done.46), channel_id=1, source_target_pairs={{0,32},{32,0},{1,33},{33,1},{2,34},{34,2},{3,35},{35,3},{4,36},{36... | collective-permute-start | bytes 7077896 | tf_op jit(solution)/shard_map/ppermute | solution.py:37
  113.5 41.0 %collective-permute-start.17 = (bf16[1152,1024]{1,0:T(8,128)(2,1)}, bf16[1152,1024]{1,0:T(8,128)(2,1)}, u32[]{:S(2)}, u32[]{:S(2)}) collective-permute-start(bf16[1152,1024]{1,0:T(8,128)(2,1)} %pad_maximum_fusion.2.rest_3_), channel_id=1, source_target_pairs={{0,32},{32,0},{1,33},{33,1},{2,34},{34,2},{3,35},{35,3},{4,36},{36... | collective-permute-start | bytes 7077896 | tf_op jit(solution)/shard_map/ppermute | solution.py:37
  136.7 30.0 %collective-permute-start.20 = (bf16[1152,1024]{1,0:T(8,128)(2,1)}, bf16[1152,1024]{1,0:T(8,128)(2,1)}, u32[]{:S(2)}, u32[]{:S(2)}) collective-permute-start(bf16[1152,1024]{1,0:T(8,128)(2,1)} %collective-permute-done.12.rest_6_), channel_id=1, source_target_pairs={{0,32},{32,0},{1,33},{33,1},{2,34},{34,2},{3,35},{35,3},{4,36},{36... | collective-permute-start | bytes 7077896 | tf_op jit(solution)/shard_map/ppermute | solution.py:37
  137.2 29.4 %collective-permute-start.21 = (bf16[1152,1024]{1,0:T(8,128)(2,1)}, bf16[1152,1024]{1,0:T(8,128)(2,1)}, u32[]{:S(2)}, u32[]{:S(2)}) collective-permute-start(bf16[1152,1024]{1,0:T(8,128)(2,1)} %collective-permute-done.13.rest_7_), channel_id=1, source_target_pairs={{0,32},{32,0},{1,33},{33,1},{2,34},{34,2},{3,35},{35,3},{4,36},{36... | collective-permute-start | bytes 7077896 | tf_op jit(solution)/shard_map/ppermute | solution.py:37
  196.5 20.8 %all-to-all-start.2 = ((bf16[8,256,128]{2,1,0:T(8,128)(2,1)}), bf16[8,256,128]{2,1,0:T(8,128)(2,1)}, u32[]{:S(2)}, u32[]{:S(2)}) async-start(bf16[8,256,128]{2,1,0:T(8,128)(2,1)} %bitcast.181), calls=%async_computation.2 | async-start | bytes 1048576 | tf_op jit(solution)/shard_map/all_to_all | solution.py:655
  200.6 145.8 %reduce-scatter.2.cloned.1.call-start = ((), (), s32[]{:S(2)}) async-start(), calls=%async_computation.6 | async-start | bytes 12255232 | tf_op jit(solution)/shard_map/reduce_scatter | solution.py:79
  245.5 36.3 %collective-permute-start.24 = (bf16[8,2,128,128]{3,2,1,0:T(8,128)(2,1)}, bf16[8,2,128,128]{3,2,1,0:T(8,128)(2,1)}, u32[]{:S(2)}, u32[]{:S(2)}) collective-permute-start(bf16[8,2,128,128]{3,2,1,0:T(8,128)(2,1)} %get-tuple-element.96), channel_id=1, source_target_pairs={{0,2},{2,4},{4,6},{6,0},{1,3},{3,5},{5,7},{7,1},{8,10},{10,12},{12... | collective-permute-start | bytes 1572872 | tf_op jit(solution)/shard_map/ppermute | solution.py:33
  247.0 34.8 %collective-permute-start.25 = (bf16[8,2,128,128]{3,2,1,0:T(8,128)(2,1)}, bf16[8,2,128,128]{3,2,1,0:T(8,128)(2,1)}, u32[]{:S(2)}, u32[]{:S(2)}) collective-permute-start(bf16[8,2,128,128]{3,2,1,0:T(8,128)(2,1)} %get-tuple-element.98), channel_id=1, source_target_pairs={{0,6},{2,0},{4,2},{6,4},{1,7},{3,1},{5,3},{7,5},{8,14},{10,8},{12,... | collective-permute-start | bytes 1572872 | tf_op jit(solution)/shard_map/ppermute | solution.py:33
  255.6 39.6 %collective-permute-start.26 = (bf16[8,2,128,128]{3,2,1,0:T(8,128)(2,1)}, bf16[8,2,128,128]{3,2,1,0:T(8,128)(2,1)}, u32[]{:S(2)}, u32[]{:S(2)}) collective-permute-start(bf16[8,2,128,128]{3,2,1,0:T(8,128)(2,1)} %get-tuple-element.97), channel_id=1, source_target_pairs={{0,4},{2,6},{4,0},{6,2},{1,5},{3,7},{5,1},{7,3},{8,12},{10,14},{12... | collective-permute-start | bytes 1572872 | tf_op jit(solution)/shard_map/ppermute | solution.py:33
  361.2 122.0 %all-to-all-start.4 = ((bf16[16,32,4352]{2,1,0:T(8,128)(2,1)}), bf16[16,32,4352]{2,1,0:T(8,128)(2,1)}, u32[]{:S(2)}, u32[]{:S(2)}) async-start(bf16[16,32,4352]{2,1,0:T(8,128)(2,1)} %bitcast.180), calls=%async_computation.5 | async-start | bytes 8912896 | tf_op jit(solution)/shard_map/all_to_all | solution.py:84
  369.1 63.4 %collective-permute-start.50 = (bf16[16,5632]{1,0:T(8,128)(2,1)S(1)}, bf16[16,5632]{1,0:T(8,128)(2,1)S(1)}, u32[]{:S(2)}, u32[]{:S(2)}) collective-permute-start(bf16[16,5632]{1,0:T(8,128)(2,1)S(1)} %get-tuple-element.82), channel_id=1, source_target_pairs={{0,2},{2,4},{4,6},{6,0},{1,3},{3,5},{5,7},{7,1},{8,10},{10,12},{12... | collective-permute-start | bytes 540680 | tf_op jit(solution)/shard_map/ppermute | solution.py:33
  371.2 66.9 %collective-permute-start.51 = (bf16[16,5632]{1,0:T(8,128)(2,1)S(1)}, bf16[16,5632]{1,0:T(8,128)(2,1)S(1)}, u32[]{:S(2)}, u32[]{:S(2)}) collective-permute-start(bf16[16,5632]{1,0:T(8,128)(2,1)S(1)} %get-tuple-element.82), channel_id=1, source_target_pairs={{0,6},{2,0},{4,2},{6,4},{1,7},{3,1},{5,3},{7,5},{8,14},{10,8},{12,... | collective-permute-start | bytes 540680 | tf_op jit(solution)/shard_map/ppermute | solution.py:33
  372.4 68.0 %collective-permute-start.52 = (bf16[16,5632]{1,0:T(8,128)(2,1)S(1)}, bf16[16,5632]{1,0:T(8,128)(2,1)S(1)}, u32[]{:S(2)}, u32[]{:S(2)}) collective-permute-start(bf16[16,5632]{1,0:T(8,128)(2,1)S(1)} %get-tuple-element.82), channel_id=1, source_target_pairs={{0,4},{2,6},{4,0},{6,2},{1,5},{3,7},{5,1},{7,3},{8,12},{10,14},{12... | collective-permute-start | bytes 540680 | tf_op jit(solution)/shard_map/ppermute | solution.py:33
  374.8 69.0 %collective-permute-start.56 = (bf16[16,5632]{1,0:T(8,128)(2,1)S(1)}, bf16[16,5632]{1,0:T(8,128)(2,1)S(1)}, u32[]{:S(2)}, u32[]{:S(2)}) collective-permute-start(bf16[16,5632]{1,0:T(8,128)(2,1)S(1)} %get-tuple-element.80), channel_id=1, source_target_pairs={{0,8},{8,16},{16,24},{24,0},{1,9},{9,17},{17,25},{25,1},{2,10},{10... | collective-permute-start | bytes 540680 | tf_op jit(solution)/shard_map/ppermute | solution.py:33
  376.3 69.7 %collective-permute-start.57 = (bf16[16,5632]{1,0:T(8,128)(2,1)S(1)}, bf16[16,5632]{1,0:T(8,128)(2,1)S(1)}, u32[]{:S(2)}, u32[]{:S(2)}) collective-permute-start(bf16[16,5632]{1,0:T(8,128)(2,1)S(1)} %get-tuple-element.80), channel_id=1, source_target_pairs={{0,24},{8,0},{16,8},{24,16},{1,25},{9,1},{17,9},{25,17},{2,26},{10... | collective-permute-start | bytes 540680 | tf_op jit(solution)/shard_map/ppermute | solution.py:33
  440.5 20.2 %collective-permute-start.53 = (bf16[4,16,5632]{2,1,0:T(8,128)(2,1)S(1)}, bf16[4,16,5632]{2,1,0:T(8,128)(2,1)S(1)}, u32[]{:S(2)}, u32[]{:S(2)}) collective-permute-start(bf16[4,16,5632]{2,1,0:T(8,128)(2,1)S(1)} %bitcast_dynamic-update-slice_fusion.4), channel_id=1, source_target_pairs={{0,8},{8,16},{16,24},{24,0},{1,9},{9,17},{17,25},{25,1},{2,10},{10... | collective-permute-start | bytes 2162696 | tf_op jit(solution)/shard_map/ppermute | solution.py:33
  440.7 31.8 %collective-permute-start.54 = (bf16[4,16,5632]{2,1,0:T(8,128)(2,1)S(1)}, bf16[4,16,5632]{2,1,0:T(8,128)(2,1)S(1)}, u32[]{:S(2)}, u32[]{:S(2)}) collective-permute-start(bf16[4,16,5632]{2,1,0:T(8,128)(2,1)S(1)} %bitcast_dynamic-update-slice_fusion.4), channel_id=1, source_target_pairs={{0,24},{8,0},{16,8},{24,16},{1,25},{9,1},{17,9},{25,17},{2,26},{10... | collective-permute-start | bytes 2162696 | tf_op jit(solution)/shard_map/ppermute | solution.py:33
  443.8 29.5 %collective-permute-start.55 = (bf16[4,16,5632]{2,1,0:T(8,128)(2,1)S(1)}, bf16[4,16,5632]{2,1,0:T(8,128)(2,1)S(1)}, u32[]{:S(2)}, u32[]{:S(2)}) collective-permute-start(bf16[4,16,5632]{2,1,0:T(8,128)(2,1)S(1)} %bitcast_dynamic-update-slice_fusion.4), channel_id=1, source_target_pairs={{0,16},{8,24},{16,0},{24,8},{1,17},{9,25},{17,1},{25,9},{2,18},{10... | collective-permute-start | bytes 2162696 | tf_op jit(solution)/shard_map/ppermute | solution.py:33
  446.1 31.6 %collective-permute-start.59 = (bf16[4,16,5632]{2,1,0:T(8,128)(2,1)S(1)}, bf16[4,16,5632]{2,1,0:T(8,128)(2,1)S(1)}, u32[]{:S(2)}, u32[]{:S(2)}) collective-permute-start(bf16[4,16,5632]{2,1,0:T(8,128)(2,1)S(1)} %bitcast_dynamic-update-slice_fusion), channel_id=1, source_target_pairs={{0,2},{2,4},{4,6},{6,0},{1,3},{3,5},{5,7},{7,1},{8,10},{10,12},{12... | collective-permute-start | bytes 2162696 | tf_op jit(solution)/shard_map/ppermute | solution.py:33
  446.1 31.6 %collective-permute-start.60 = (bf16[4,16,5632]{2,1,0:T(8,128)(2,1)S(1)}, bf16[4,16,5632]{2,1,0:T(8,128)(2,1)S(1)}, u32[]{:S(2)}, u32[]{:S(2)}) collective-permute-start(bf16[4,16,5632]{2,1,0:T(8,128)(2,1)S(1)} %bitcast_dynamic-update-slice_fusion), channel_id=1, source_target_pairs={{0,6},{2,0},{4,2},{6,4},{1,7},{3,1},{5,3},{7,5},{8,14},{10,8},{12,... | collective-permute-start | bytes 2162696 | tf_op jit(solution)/shard_map/ppermute | solution.py:33
  460.7 19.1 %collective-permute-start.61 = (bf16[4,16,5632]{2,1,0:T(8,128)(2,1)S(1)}, bf16[4,16,5632]{2,1,0:T(8,128)(2,1)S(1)}, u32[]{:S(2)}, u32[]{:S(2)}) collective-permute-start(bf16[4,16,5632]{2,1,0:T(8,128)(2,1)S(1)} %bitcast_dynamic-update-slice_fusion), channel_id=1, source_target_pairs={{0,4},{2,6},{4,0},{6,2},{1,5},{3,7},{5,1},{7,3},{8,12},{10,14},{12... | collective-permute-start | bytes 2162696 | tf_op jit(solution)/shard_map/ppermute | solution.py:33
  (86 other events, 666.4 us)
Sparse Core Ops, SparseCore 0:
  217.4 127.0 reduce-scatter.1
